TPU v7x, 512 devices: a whole 4x4x16 slice. The times are simulated.
512 devices in a mesh: group: 16 (over x, y_hi, core), brick: 32 (over y_lo, z).
Axes of the slice: x: 4, y: 4 (y_hi: 2, y_lo: 2; y = y_hi * 2 + y_lo), z: 16, core: 2. Of those that a mesh axis runs over, the one named last changes fastest.
Arguments:
- field: float32 [32, 128, 16, 128], P('group', 'brick'), may hold values from -6 to 6
- cotangent: float32 [32, 128, 16, 128], P('group', 'brick'), may hold values from -6 to 6
- w_fine: bfloat16 [27, 128, 128], replicated, may hold values from -0.109375 to 0.109375
- w_coarse: bfloat16 [27, 128, 128], replicated, may hold values from -0.3125 to 0.3125
Outputs:
- output: float32 [32, 128, 16, 128], P('group', 'brick')
- grad_fine: float32 [27, 128, 128], P(None, 'brick')
- grad_coarse: float32 [27, 128, 128], P(None, 'brick')
All inputs are finite; a program needn't handle non-finite values.
Results may differ from a plain program's by a relative error of at most 0.0053.
Values may be sent and summed in bfloat16 or wider, within the bound.
A program may use at most 64 MiB of HBM per device.

v0:
```python
import jax
import jax.numpy as jnp
from jax import lax
from jax.sharding import PartitionSpec as P


def extended(cells, sides, width):
    for axis, dim in sides:
        count = lax.axis_size(axis)
        ends = count - 1
        head = lax.slice_in_dim(cells, 0, width, axis=dim)
        tail = lax.slice_in_dim(cells, cells.shape[dim] - width, cells.shape[dim], axis=dim)
        cells = jnp.concatenate(
            [
                lax.ppermute(tail, axis, [(i, (i + 1) % count) for i in range(ends)]),
                cells,
                lax.ppermute(head, axis, [((i + 1) % count, i) for i in range(ends)]),
            ],
            axis=dim,
        )
    return cells


def conv_padded(padded, weights):
    size_x = padded.shape[0] - 2
    size_y = padded.shape[1] - 2
    size_z = padded.shape[2] - 2
    channels = padded.shape[3]
    total = jnp.zeros((size_x * size_y * size_z, weights.shape[2]), jnp.float32)
    for offset in range(27):
        step_x, step_y, step_z = (offset // 9, offset // 3 % 3, offset % 3)
        window = padded[
            step_x : step_x + size_x, step_y : step_y + size_y, step_z : step_z + size_z
        ].reshape(-1, channels)
        total = total + jnp.dot(window, weights[offset], preferred_element_type=jnp.float32)
    return total.reshape(size_x, size_y, size_z, -1)


def transposed(padded, weights):
    size_x = padded.shape[0] - 2
    size_y = padded.shape[1] - 2
    size_z = padded.shape[2] - 2
    channels = padded.shape[3]
    total = jnp.zeros((size_x * size_y * size_z, weights.shape[1]), jnp.float32)
    for offset in range(27):
        step_x, step_y, step_z = (2 - offset // 9, 2 - offset // 3 % 3, 2 - offset % 3)
        window = padded[
            step_x : step_x + size_x, step_y : step_y + size_y, step_z : step_z + size_z
        ].reshape(-1, channels)
        total = total + lax.dot_general(
            window, weights[offset], (((1,), (1,)), ((), ())), preferred_element_type=jnp.float32
        )
    return total.reshape(size_x, size_y, size_z, -1)


def weight_grad(padded, grads):
    size_x, size_y, size_z, outputs = grads.shape
    channels = padded.shape[3]
    flat = grads.reshape(-1, outputs)
    pieces = []
    for offset in range(27):
        step_x, step_y, step_z = (offset // 9, offset // 3 % 3, offset % 3)
        window = padded[
            step_x : step_x + size_x, step_y : step_y + size_y, step_z : step_z + size_z
        ].reshape(-1, channels)
        pieces.append(
            lax.dot_general(
                window, flat, (((0,), (0,)), ((), ())), preferred_element_type=jnp.float32
            )
        )
    return jnp.stack(pieces)


def dsilu(values):
    sig = jax.nn.sigmoid(values)
    return sig * (1.0 + values * (1.0 - sig))


def pad_depth(values):
    return jnp.pad(values, ((0, 0), (0, 0), (1, 1), (0, 0)))


def pad_sides(values):
    return jnp.pad(values, ((0, 0), (1, 1), (1, 1), (0, 0)))


def block_sum(values):
    size_x, size_y, size_z, channels = values.shape
    shaped = values.reshape(size_x // 2, 2, size_y // 2, 2, size_z // 2, 2, channels)
    return jnp.sum(shaped, axis=(1, 3, 5))


def expand(values):
    size_x, size_y, size_z, channels = values.shape
    wide = jnp.broadcast_to(
        values[:, None, :, None, :, None, :], (size_x, 2, size_y, 2, size_z, 2, channels)
    )
    return wide.reshape(2 * size_x, 2 * size_y, 2 * size_z, channels)


def body(field, cotangent, w_fine, w_coarse):
    fine_b = field.astype(jnp.bfloat16)
    fine_pad = pad_depth(extended(fine_b, (("group", 0), ("brick", 1)), 1))
    z_fine = conv_padded(fine_pad, w_fine)
    act_fine = jax.nn.silu(z_fine)
    coarse = (block_sum(act_fine) * 0.125).astype(jnp.bfloat16)
    rows = coarse.shape[1]
    channels = coarse.shape[3]
    brick_pos = lax.axis_index("brick")
    share = channels // lax.axis_size("brick")
    block = lax.all_gather(coarse, "brick", axis=1, tiled=True)
    block_pad = pad_sides(extended(block, (("group", 0),), 1))
    z_block = conv_padded(block_pad, w_coarse)
    z_coarse = lax.dynamic_slice_in_dim(z_block, brick_pos * rows, rows, 1)
    act_coarse = jax.nn.silu(z_coarse)
    output = act_fine + expand(act_coarse)
    d_coarse = block_sum(cotangent)
    g_coarse = (d_coarse * dsilu(z_coarse)).astype(jnp.bfloat16)
    grad_block = lax.all_gather(g_coarse, "brick", axis=1, tiled=True)
    grad_pad = pad_sides(extended(grad_block, (("group", 0),), 1))
    own_pad = lax.dynamic_slice_in_dim(grad_pad, brick_pos * rows, rows + 2, 1)
    own_inputs = lax.dynamic_slice_in_dim(block_pad, brick_pos * share, share, 3)
    own_grad = weight_grad(own_inputs, grad_block)
    empty = jnp.zeros((27, channels, w_coarse.shape[2]), jnp.float32)
    grad_coarse = lax.dynamic_update_slice_in_dim(empty, own_grad, brick_pos * share, 1)
    back_coarse = transposed(own_pad, w_coarse)
    g_fine = ((cotangent + expand(back_coarse) * 0.125) * dsilu(z_fine)).astype(jnp.bfloat16)
    grad_fine = weight_grad(fine_pad, g_fine)
    share_fine, share_coarse = (
        lax.psum_scatter(grad_fine, "brick", scatter_dimension=1, tiled=True),
        lax.psum_scatter(grad_coarse, "brick", scatter_dimension=1, tiled=True),
    )
    sum_fine, sum_coarse = lax.psum((share_fine, share_coarse), "group")
    return (output, sum_fine, sum_coarse)


def solution(mesh):
    in_specs = (P("group", "brick", None, None), P("group", "brick", None, None), P(), P())
    out_specs = (P("group", "brick", None, None), P(None, "brick", None), P(None, "brick", None))
    return jax.shard_map(body, mesh=mesh, in_specs=in_specs, out_specs=out_specs, check_vma=False)
```

profile of v0, /device:TPU:1, one launch (start us, length us, event | category | flops | bytes accessed | tf_op | source)
XLA Modules:
  0.0 692.3 jit_solution(3883432672535617534)
XLA Ops:
  8.1 6.2 collective-permute-start
  14.4 3.9 collective-permute-start.1
  20.9 3.5 collective-permute-start.2
  25.8 3.3 collective-permute-done.3
  33.3 52.6 %all-gather = bf16[64,8,128]{2,1,0:T(8,128)(2,1)S(1)} all-gather(bf16[2,8,128]{2,1,0:T(8,128)(2,1)S(1)} %multiply_convert_fusion.1), channel_id=2, replica_groups=mesh['group'=16,'brick'=32] {'brick'}, dimensions={0}, use_global_device_ids=true | all-gather | bytes 135168 | tf_op jit(solution)/shard_map/all_gather | solution.py:111
  86.1 17.7 %collective-permute-start.4 = (bf16[1,64,8,128]{1,3,2,0:T(8,128)(2,1)S(1)}, bf16[1,64,8,128]{1,3,2,0:T(8,128)(2,1)S(1)}, u32[]{:S(2)}, u32[]{:S(2)}) collective-permute-start(bf16[1,64,8,128]{1,3,2,0:T(8,128)(2,1)S(1)} %bitcast.979), channel_id=1, source_target_pairs={{0,32},{32,64},{64,96},{96,128},{128,160},{160,192},{192,224},{224... | collective-permute-start | bytes 393224 | tf_op jit(solution)/shard_map/ppermute | solution.py:15
  103.8 1.9 collective-permute-start.5
  107.1 5.9 collective-permute-done.5
  114.9 2.8 fusion.383
  117.7 1.8 copy.134
  119.6 1.7 copy.135
  121.3 1.7 copy.136
  123.0 1.7 copy.137
  126.5 1.8 fusion.128
  128.3 1.8 fusion.122
  131.8 1.7 copy.141
  133.5 1.7 copy.142
  135.3 1.7 copy.143
  137.0 1.7 copy.144
  144.5 1.8 convolution_add_fusion.21
  146.3 1.7 copy.138
  153.4 1.7 copy.147
  155.2 1.7 copy.148
  156.9 1.7 copy.149
  160.4 1.8 copy.151
  163.9 1.7 copy.153
  165.6 1.8 copy.154
  173.9 45.3 %all_gather.7 = bf16[1,64,8,128]{3,2,0,1:T(8,128)(2,1)S(1)} all-gather(bf16[1,2,8,128]{3,2,0,1:T(8,128)(2,1)S(1)} %get-tuple-element.31), channel_id=1, replica_groups=mesh['group'=16,'brick'=32] {'brick'}, dimensions={1}, use_global_device_ids=true | all-gather | bytes 135168 | tf_op jit(solution)/shard_map/all_gather | solution.py:119
  219.2 15.7 %collective-permute-start.6 = (bf16[1,64,8,128]{3,2,1,0:T(8,128)(2,1)S(1)}, bf16[1,64,8,128]{3,2,1,0:T(8,128)(2,1)S(1)}, u32[]{:S(2)}, u32[]{:S(2)}) collective-permute-start(bf16[1,64,8,128]{3,2,1,0:T(8,128)(2,1)S(1)} %bitcast.975), channel_id=1, source_target_pairs={{0,32},{32,64},{64,96},{96,128},{128,160},{160,192},{192,224},{224... | collective-permute-start | bytes 393224 | tf_op jit(solution)/shard_map/ppermute | solution.py:15
  234.9 2.1 collective-permute-start.7
  274.0 242.8 %all-reduce.10.cloned.1.call-done = (f32[27,128,128]{2,1,0:T(8,128)}, f32[27,128,128]{2,1,0:T(8,128)}) async-done(((f32[27,128,128]{2,1,0:T(8,128)}, f32[27,128,128]{2,1,0:T(8,128)}), (f32[27,128,128]{2,1,0:T(8,128)}, f32[27,128,128]{2,1,0:T(8,128)})) %all-reduce.10.cloned.1.call-update) | async-done | bytes 3538960
  519.8 162.7 %all-reduce.12.cloned.1.call-done = (f32[27,4,128]{2,1,0:T(4,128)}, f32[27,4,128]{2,1,0:T(4,128)}) async-done(((f32[27,4,128]{2,1,0:T(4,128)}, f32[27,4,128]{2,1,0:T(4,128)}), (f32[27,4,128]{2,1,0:T(4,128)}, f32[27,4,128]{2,1,0:T(4,128)})) %all-reduce.12.cloned.1.call-update) | async-done | bytes 110608 | tf_op jit(solution)/shard_map/psum | solution.py:133
  (238 shorter events, 78.7 us)
Async XLA Ops:
  7.2 22.2 %copy-start.5 = (bf16[27,128,128]{2,1,0:T(8,128)(2,1)S(1)}, bf16[27,128,128]{2,1,0:T(8,128)(2,1)}, u32[]{:S(2)}) copy-start(bf16[27,128,128]{2,1,0:T(8,128)(2,1)} %param.6) | copy-start | bytes 2654212
  7.2 509.6 %all-reduce.10.cloned.1.call-start = ((), (), s32[]{:S(2)}) async-start(), calls=%async_computation | async-start | bytes 7077888
  8.1 11.6 %collective-permute-start = (bf16[1,4,16,128]{3,2,1,0:T(8,128)(2,1)S(1)}, bf16[1,4,16,128]{3,2,1,0:T(8,128)(2,1)S(1)}, u32[]{:S(2)}, u32[]{:S(2)}) collective-permute-start(bf16[1,4,16,128]{3,2,1,0:T(8,128)(2,1)S(1)} %get-tuple-element.65), channel_id=1, source_target_pairs={{0,32},{32,64},{64,96},{96,128},{128,160},{160,192},{192,224},{224... | collective-permute-start | bytes 49160 | tf_op jit(solution)/shard_map/ppermute | solution.py:15
  14.4 6.6 collective-permute-start.1
  19.7 10.6 %copy-start.19 = (bf16[1,4,16,128]{3,2,1,0:T(8,128)(2,1)}, bf16[1,4,16,128]{3,2,1,0:T(8,128)(2,1)S(1)}, u32[]{:S(2)}) copy-start(bf16[1,4,16,128]{3,2,1,0:T(8,128)(2,1)S(1)} %collective-permute-done) | copy-start | bytes 49156
  20.9 9.4 %copy-start.21 = (bf16[1,4,16,128]{3,2,1,0:T(8,128)(2,1)}, bf16[1,4,16,128]{3,2,1,0:T(8,128)(2,1)S(1)}, u32[]{:S(2)}) copy-start(bf16[1,4,16,128]{3,2,1,0:T(8,128)(2,1)S(1)} %collective-permute-done.1) | copy-start | bytes 49156
  20.9 4.9 collective-permute-start.2
  24.5 4.7 collective-permute-start.3
  25.8 4.7 copy-start.25
  86.1 21.0 %collective-permute-start.4 = (bf16[1,64,8,128]{1,3,2,0:T(8,128)(2,1)S(1)}, bf16[1,64,8,128]{1,3,2,0:T(8,128)(2,1)S(1)}, u32[]{:S(2)}, u32[]{:S(2)}) collective-permute-start(bf16[1,64,8,128]{1,3,2,0:T(8,128)(2,1)S(1)} %bitcast.979), channel_id=1, source_target_pairs={{0,32},{32,64},{64,96},{96,128},{128,160},{160,192},{192,224},{224... | collective-permute-start | bytes 393224 | tf_op jit(solution)/shard_map/ppermute | solution.py:15
  103.8 9.2 %collective-permute-start.5 = (bf16[1,64,8,128]{1,3,2,0:T(8,128)(2,1)S(1)}, bf16[1,64,8,128]{1,3,2,0:T(8,128)(2,1)S(1)}, u32[]{:S(2)}, u32[]{:S(2)}) collective-permute-start(bf16[1,64,8,128]{1,3,2,0:T(8,128)(2,1)S(1)} %bitcast.980), channel_id=1, source_target_pairs={{32,0},{64,32},{96,64},{128,96},{160,128},{192,160},{224,192},{256... | collective-permute-start | bytes 393224 | tf_op jit(solution)/shard_map/ppermute | solution.py:17
  107.1 6.4 copy-start.2
  117.7 8.8 %copy-start.1 = (bf16[27,128,128]{2,1,0:T(8,128)(2,1)S(1)}, bf16[27,128,128]{2,1,0:T(8,128)(2,1)}, u32[]{:S(2)}) copy-start(bf16[27,128,128]{2,1,0:T(8,128)(2,1)} %param.7) | copy-start | bytes 2654212
  148.0 3.6 copy-start.14
  148.1 3.8 copy-start.12
  148.1 4.0 copy-start.10
  149.4 2.8 copy-start.8
  167.5 2.0 copy-start.3
  169.2 3.0 copy-start.15
  169.4 2.5 copy-start.17
  169.6 2.5 copy-start.16
  169.6 2.8 copy-start.13
  170.7 1.9 copy-start.11
  219.2 25.0 %collective-permute-start.6 = (bf16[1,64,8,128]{3,2,1,0:T(8,128)(2,1)S(1)}, bf16[1,64,8,128]{3,2,1,0:T(8,128)(2,1)S(1)}, u32[]{:S(2)}, u32[]{:S(2)}) collective-permute-start(bf16[1,64,8,128]{3,2,1,0:T(8,128)(2,1)S(1)} %bitcast.975), channel_id=1, source_target_pairs={{0,32},{32,64},{64,96},{96,128},{128,160},{160,192},{192,224},{224... | collective-permute-start | bytes 393224 | tf_op jit(solution)/shard_map/ppermute | solution.py:15
  234.9 9.3 %collective-permute-start.7 = (bf16[1,64,8,128]{3,2,1,0:T(8,128)(2,1)S(1)}, bf16[1,64,8,128]{3,2,1,0:T(8,128)(2,1)S(1)}, u32[]{:S(2)}, u32[]{:S(2)}) collective-permute-start(bf16[1,64,8,128]{3,2,1,0:T(8,128)(2,1)S(1)} %bitcast.976), channel_id=1, source_target_pairs={{32,0},{64,32},{96,64},{128,96},{160,128},{192,160},{224,192},{256... | collective-permute-start | bytes 393224 | tf_op jit(solution)/shard_map/ppermute | solution.py:17
  244.0 5.4 copy-start.18
  244.0 6.9 copy-start.20
  244.0 6.9 copy-start.22
  244.0 6.9 copy-start.26
  244.2 9.9 %copy-start = (f32[27,128,128]{2,1,0:T(8,128)}, f32[27,128,128]{2,1,0:T(8,128)S(1)}, u32[]{:S(2)}) copy-start(f32[27,128,128]{2,1,0:T(8,128)S(1)} %constant_dynamic-update-slice_fusion) | copy-start | bytes 5308420
  245.2 10.5 %copy-start.24 = (bf16[4,1,16,128]{3,2,1,0:T(8,128)(2,1)S(1)}, bf16[4,1,16,128]{3,2,1,0:T(8,128)(2,1)}, u32[]{:S(2)}) copy-start(bf16[4,1,16,128]{3,2,1,0:T(8,128)(2,1)} %copy-done.23) | copy-start | bytes 49156
  272.0 410.6 %all-reduce.12.cloned.1.call-start = ((), (), s32[]{:S(2)}) async-start(), calls=%async_computation.1 | async-start | bytes 221184 | tf_op jit(solution)/shard_map/psum | solution.py:133
  (6 other events, 7.2 us)
Sparse Core Ops, SparseCore 0:
  272.1 244.5 all-reduce.9
  520.6 161.9 all-reduce.11
where the time goes:
time: 694 us; the launch traced here: 692 us
  waiting for transfers between devices  416 us (60%)
  blocking collectives  97.8 us (14%)
  matrix products  54.2 us (8%)
  starting transfers between devices  52.5 us (8%)
  local copies, waits for them, and re-layouts  50.2 us (7%)
  between operations  15.4 us (2%)
    unnamed x3, waiting for transfers between devices  243 us
    psum x1, waiting for transfers between devices, body(): sum_fine, sum_coarse = lax.psum((share_fine, share_coarse), 'group')  163 us
    all_gather x1, blocking collectives, body(): block = lax.all_gather(coarse, 'brick', axis=1, tiled=True)  52.6 us
    all_gather x1, blocking collectives, body(): grad_block = lax.all_gather(g_coarse, 'brick', axis=1, tiled=True)  45.3 us
    ppermute x4, starting transfers between devices, extended(): lax.ppermute(tail, axis, [(i, (i + 1) % count) for i in range(ends)])  43.2 us
    slice x28, local copies, waits for them, and re-layouts, conv_padded(): padded[step_x:step_x + size_x, step_y:step_y + size_y, step_z:step_z + si...  40.5 us
    dot_general x54, matrix products, weight_grad(): lax.dot_general(window, flat, (((0,), (0,)), ((), ())), preferred_element...  28.8 us
    dot_general x54, matrix products, conv_padded(): jnp.dot(window, weights[offset], preferred_element_type=jnp.float32)  21.3 us
  transfers between devices with their start and end apart: 10, of which 6 were waited for; matrix products, arithmetic and copies ran while one was open for 2% of the time, Pallas kernels for 0%

commit v1 on v0

v1 whole, which is shorter than its diff:
```python
import jax
import jax.numpy as jnp
from jax import lax
from jax.experimental import pallas as pl
from jax.experimental.pallas import tpu as pltpu
from jax.sharding import PartitionSpec as P

CH = 128
GROUPS = 16
BRICKS = 32
F32 = jnp.float32
BF16 = jnp.bfloat16
PART = 7


def wait_for(ref, sem):
    pltpu.make_async_copy(ref, ref, sem).wait()


def iota(shape, dim):
    return lax.broadcasted_iota(jnp.int32, shape, dim)


def neighbours_along_depth(rows, depth):
    count = rows.shape[0]
    place = iota(rows.shape, 0) & (depth - 1)
    before = jnp.where(place == 0, 0.0, pltpu.roll(rows, 1, 0))
    after = jnp.where(place == depth - 1, 0.0, pltpu.roll(rows, count - 1, 0))
    return before, after


def matmul_nt(a, b):
    return lax.dot_general(a, b, (((1,), (1,)), ((), ())), preferred_element_type=F32)


def pooled(values, pool):
    pool[...] = jnp.sum(values.reshape(2, 2, 2, 16, CH), axis=(0, 2)).reshape(32, CH)
    return pool[pl.ds(0, 16, stride=2), :] + pool[pl.ds(1, 16, stride=2), :]


def spread(values, pool):
    pool[pl.ds(0, 16, stride=2), :] = values
    pool[pl.ds(1, 16, stride=2), :] = values
    wide = jnp.broadcast_to(pool[...].reshape(1, 2, 1, 16, CH), (2, 2, 2, 16, CH))
    return wide.reshape(128, CH)


def selection(offset, rows, size_y, size_z):
    row = iota((rows, 128), 0)
    cell = iota((rows, 128), 1)
    step_x, step_y, step_z = offset // 9, (offset // 3) % 3, offset % 3
    plane = size_y * size_z
    z = cell % size_z + step_z - 1
    y = (cell // size_z) % size_y + step_y
    x = cell // plane + step_x
    source = (x * (size_y + 2) + y) * size_z + z
    inside = (z >= 0) & (z < size_z)
    if size_y == 2:
        inside = inside & (cell < plane)
    hit = inside & (row == source) & (offset < 27)
    return jnp.where(hit, 1.0, 0.0).astype(BF16)


def kernel(
    field, cot, w_fine, w_coarse, output, grad_fine, grad_coarse,
    field_v, cot_v, out_v, wf_v, wc_v, ext, ext3, pool, cext, gext,
    et_send, et_recv, ct_send, ct_recv, lf, lc, gf, gc, acc_f, acc_c,
    rows_f, rows_c, sum_f, sum_c, fin_f, fin_c,
    local_sem, send_sem, recv_sem,
):
    g = lax.axis_index("group")
    b = lax.axis_index("brick")
    g_up, g_down = (g + 1) % GROUPS, (g + GROUPS - 1) % GROUPS
    b_up, b_down = (b + 1) % BRICKS, (b + BRICKS - 1) % BRICKS
    share, quarter = g // 4, g % 4

    loads = [
        pltpu.make_async_copy(src, dst, local_sem.at[i])
        for i, (src, dst) in enumerate(((field, field_v), (cot, cot_v), (w_fine, wf_v), (w_coarse, wc_v)))
    ]
    for load in loads:
        load.start()

    barrier = pltpu.get_barrier_semaphore()

    def greet(group, brick):
        pl.semaphore_signal(barrier, inc=1, device_id=(group, brick), device_id_type=pl.DeviceIdType.MESH)

    for group in (g_up, g_down):
        for brick in (b_up, b_down):
            greet(group, brick)
    pl.loop(1, GROUPS)(lambda i: greet((g + i) % GROUPS, b))
    pl.loop(1, BRICKS)(lambda i: greet(g, (b + i) % BRICKS))

    def send(src, dst, phase, group, brick):
        pltpu.make_async_remote_copy(
            src_ref=src,
            dst_ref=dst,
            send_sem=send_sem.at[phase],
            recv_sem=recv_sem.at[phase],
            device_id=(group, brick),
            device_id_type=pl.DeviceIdType.MESH,
        ).start()

    loads[0].wait()
    ext[1:3, 1:5] = field_v[...].astype(BF16)
    pl.semaphore_wait(barrier, 4 + GROUPS - 1 + BRICKS - 1)

    send(ext.at[1, pl.ds(1, 4)], ext.at[3, pl.ds(1, 4)], 0, g_down, b)
    send(ext.at[2, pl.ds(1, 4)], ext.at[0, pl.ds(1, 4)], 0, g_up, b)
    send(ext.at[pl.ds(1, 2), 1], ext.at[pl.ds(1, 2), 5], 0, g, b_down)
    send(ext.at[pl.ds(1, 2), 4], ext.at[pl.ds(1, 2), 0], 0, g, b_up)
    send(ext.at[1, 1], ext.at[3, 5], 0, g_down, b_down)
    send(ext.at[1, 4], ext.at[3, 0], 0, g_down, b_up)
    send(ext.at[2, 1], ext.at[0, 5], 0, g_up, b_down)
    send(ext.at[2, 4], ext.at[0, 0], 0, g_up, b_up)

    loads[1].wait()
    cot_rows = cot_v[...].reshape(128, CH)
    d_coarse = pooled(cot_rows, pool)
    order = iota((CH, CH), 0)
    sort = jnp.where(iota((CH, CH), 1) == 4 * (order % 32) + order // 32, 1.0, 0.0).astype(BF16)

    wait_for(ext.at[pl.ds(0, 4), pl.ds(0, 4)], recv_sem.at[0])

    wait_for(ext.at[pl.ds(0, 4), pl.ds(0, 4)], send_sem.at[0])

    def clear(outside, part):
        @pl.when(outside)
        def _():
            ext[part] = jnp.zeros(ext.at[part].shape, BF16)

    clear(g == 0, slice(0, 1))
    clear(g == GROUPS - 1, slice(3, 4))
    clear(b == 0, (slice(0, 4), slice(0, 1)))
    clear(b == BRICKS - 1, (slice(0, 4), slice(5, 6)))

    cells = ext[...].reshape(384, CH)
    et_send[...] = matmul_nt(sort, cells).astype(BF16).reshape(4, 32, 384)
    et_recv[0] = et_send[share]

    @pl.loop(1, GROUPS)
    def _(i):
        to = (g + i) % GROUPS
        send(et_send.at[to // 4], et_recv.at[i], 1, to, b)

    before, after = neighbours_along_depth(cells.astype(F32), 16)
    ext3[:, :, :, 0:CH] = before.astype(BF16).reshape(4, 6, 16, CH)
    ext3[:, :, :, CH : 2 * CH] = ext[...]
    ext3[:, :, :, 2 * CH :] = after.astype(BF16).reshape(4, 6, 16, CH)

    loads[2].wait()
    z_fine = jnp.zeros((128, CH), F32)
    for step in range(9):
        step_x, step_y = step // 3, step % 3
        window = ext3[step_x : step_x + 2, step_y : step_y + 4].reshape(128, 3 * CH)
        z_fine = z_fine + jnp.dot(window, wf_v[step], preferred_element_type=F32)
    sig = jax.nn.sigmoid(z_fine)
    act_fine = z_fine * sig
    slope_fine = sig * (1.0 + z_fine * (1.0 - sig))
    coarse = (pooled(act_fine, pool) * 0.125).astype(BF16).astype(F32)

    def coarse_halo(buf, phase):
        send(buf.at[pl.ds(5, 2)], buf.at[pl.ds(9, 2)], phase, g_down, b)
        send(buf.at[pl.ds(5, 2)], buf.at[pl.ds(1, 2)], phase, g_up, b)
        send(buf.at[5], buf.at[7], phase, g, b_down)
        send(buf.at[6], buf.at[4], phase, g, b_up)
        send(buf.at[5], buf.at[11], phase, g_down, b_down)
        send(buf.at[6], buf.at[8], phase, g_down, b_up)
        send(buf.at[5], buf.at[3], phase, g_up, b_down)
        send(buf.at[6], buf.at[0], phase, g_up, b_up)

    def coarse_halo_wait(buf, phase):
        wait_for(buf.at[pl.ds(0, 10)], recv_sem.at[phase])
        wait_for(buf.at[pl.ds(0, 10)], send_sem.at[phase])

        def clear(outside, rows):
            @pl.when(outside)
            def _():
                for row in rows:
                    buf[row] = jnp.zeros((8, CH), F32)

        clear(g == 0, (0, 1, 2, 3))
        clear(g == GROUPS - 1, (8, 9, 10, 11))
        clear(b == 0, (0, 4, 8))
        clear(b == BRICKS - 1, (3, 7, 11))

    cext[5:7] = coarse.reshape(2, 8, CH)
    coarse_halo(cext, 2)
    coarse_halo_wait(cext, 2)

    ccells = cext[...].reshape(96, CH)
    before, after = neighbours_along_depth(ccells, 8)
    wide = jnp.concatenate([before, ccells, after], axis=1)
    loads[3].wait()
    z_coarse = jnp.zeros((16, CH), F32)
    for step in range(9):
        start = (step // 3) * 32 + (step % 3) * 8
        window = wide[start : start + 16].astype(BF16)
        z_coarse = z_coarse + jnp.dot(window, wc_v[step], preferred_element_type=F32)
    sig = jax.nn.sigmoid(z_coarse)
    act_coarse = z_coarse * sig
    g_coarse = d_coarse * (sig * (1.0 + z_coarse * (1.0 - sig)))
    g_coarse = g_coarse.astype(BF16)
    gext[5:7] = g_coarse.astype(F32).reshape(2, 8, CH)
    coarse_halo(gext, 3)
    gc[0] = g_coarse

    @pl.loop(1, GROUPS)
    def _(i):
        send(gc.at[0], gc.at[i], 4, (g + i) % GROUPS, b)

    ccells = jnp.concatenate([ccells, jnp.zeros((32, CH), F32)], axis=0).astype(BF16)
    ct_send[...] = matmul_nt(sort, ccells).astype(BF16).reshape(4, 32, 128)
    ct_recv[0] = ct_send[share]

    @pl.loop(1, GROUPS)
    def _(i):
        to = (g + i) % GROUPS
        send(ct_send.at[to // 4], ct_recv.at[i], 5, to, b)

    out_v[...] = (act_fine + spread(act_coarse, pool)).reshape(2, 4, 16, CH)
    store = pltpu.make_async_copy(out_v, output, local_sem.at[4])
    store.start()

    coarse_halo_wait(gext, 3)
    gcells = gext[...].reshape(96, CH)
    mixed = jnp.zeros((16, 3 * CH), F32)
    for step in range(9):
        start = (2 - step // 3) * 32 + (2 - step % 3) * 8
        window = gcells[start : start + 16].astype(BF16)
        mixed = mixed + matmul_nt(window, wc_v[step])
    back_coarse = mixed[:, CH : 2 * CH]
    back_coarse = back_coarse + neighbours_along_depth(mixed[:, 0:CH], 8)[1]
    back_coarse = back_coarse + neighbours_along_depth(mixed[:, 2 * CH :], 8)[0]
    g_fine = (cot_v[...].reshape(128, CH) + spread(back_coarse, pool) * 0.125) * slope_fine
    gf[0] = g_fine.astype(BF16)

    @pl.loop(1, GROUPS)
    def _(i):
        send(gf.at[0], gf.at[i], 6, (g + i) % GROUPS, b)

    wait_for(et_recv.at[pl.ds(0, GROUPS - 1)], recv_sem.at[1])
    everyone = et_recv[...].reshape(GROUPS * 32, 384)
    for k in range(PART):
        picked = jnp.dot(everyone, selection(quarter * PART + k, 384, 4, 16), preferred_element_type=F32)
        lf[:, k] = picked.astype(BF16).reshape(GROUPS, 32, 128)
    wait_for(ct_recv.at[pl.ds(0, GROUPS - 1)], recv_sem.at[5])
    everyone = ct_recv[...].reshape(GROUPS * 32, 128)
    for k in range(PART):
        picked = jnp.dot(everyone, selection(quarter * PART + k, 128, 2, 8), preferred_element_type=F32)
        lc[:, k] = picked.astype(BF16).reshape(GROUPS, 32, 128)

    def scatter(acc, rows, sums, total, phase):
        acc[0 : PART * 32] = total
        acc[PART * 32 :] = jnp.zeros((32, CH), F32)
        for brick in range(BRICKS):
            rows[brick] = acc[pl.ds(brick, 8, stride=32), :]
        sums[0] = rows[b]

        @pl.loop(1, BRICKS)
        def _(i):
            to = (b + i) % BRICKS
            send(rows.at[to], sums.at[i], phase, g, to)

    def gather(sums, fin, phase, after):
        wait_for(sums.at[pl.ds(0, BRICKS - 1)], recv_sem.at[phase])
        fin[g] = jnp.sum(sums[...], axis=0)

        @pl.loop(1, GROUPS)
        def _(i):
            send(fin.at[g], fin.at[g], after, (g + i) % GROUPS, b)

    wait_for(gc.at[pl.ds(0, GROUPS - 1)], recv_sem.at[4])
    total = jnp.zeros((PART * 32, CH), F32)
    for member in range(GROUPS):
        grads = jnp.concatenate([gc[member], jnp.zeros((112, CH), BF16)], axis=0)
        total = total + jnp.dot(lc[member].reshape(PART * 32, 128), grads, preferred_element_type=F32)
    scatter(acc_c, rows_c, sum_c, total, 7)

    wait_for(gf.at[pl.ds(0, GROUPS - 1)], recv_sem.at[6])
    total = jnp.zeros((PART * 32, CH), F32)
    for member in range(GROUPS):
        total = total + jnp.dot(lf[member].reshape(PART * 32, 128), gf[member], preferred_element_type=F32)
    scatter(acc_f, rows_f, sum_f, total, 8)

    gather(sum_c, fin_c, 7, 9)
    gather(sum_f, fin_f, 8, 10)

    def place(fin, grad, phase):
        wait_for(fin.at[pl.ds(0, GROUPS - 1)], recv_sem.at[phase])
        for member in range(GROUPS):
            channel, part = member // 4, member % 4
            count = PART if part < 3 else PART - 1
            grad[pl.ds(part * PART * 4 + channel, count, stride=4), :] = fin[member, 0:count]

    place(fin_c, grad_coarse, 9)
    place(fin_f, grad_fine, 10)

    wait_for(et_recv.at[pl.ds(0, GROUPS - 1)], send_sem.at[1])
    wait_for(gc.at[pl.ds(0, GROUPS - 1)], send_sem.at[4])
    wait_for(ct_recv.at[pl.ds(0, GROUPS - 1)], send_sem.at[5])
    wait_for(gf.at[pl.ds(0, GROUPS - 1)], send_sem.at[6])
    wait_for(sum_c.at[pl.ds(0, BRICKS - 1)], send_sem.at[7])
    wait_for(sum_f.at[pl.ds(0, BRICKS - 1)], send_sem.at[8])
    wait_for(fin_c.at[pl.ds(0, GROUPS - 1)], send_sem.at[9])
    wait_for(fin_f.at[pl.ds(0, GROUPS - 1)], send_sem.at[10])
    store.wait()


def body(field, cotangent, w_fine, w_coarse):
    anywhere = pl.BlockSpec(memory_space=pl.ANY)
    vmem = pl.BlockSpec(memory_space=pltpu.VMEM)
    fine = (2, 4, 16, CH)
    output, grad_fine, grad_coarse = pl.pallas_call(
        kernel,
        out_shape=(
            jax.ShapeDtypeStruct(fine, F32),
            jax.ShapeDtypeStruct((27 * 4, CH), F32),
            jax.ShapeDtypeStruct((27 * 4, CH), F32),
        ),
        in_specs=[anywhere] * 4,
        out_specs=(anywhere, vmem, vmem),
        scratch_shapes=[
            pltpu.VMEM(fine, F32),
            pltpu.VMEM(fine, F32),
            pltpu.VMEM(fine, F32),
            pltpu.VMEM((9, 3 * CH, CH), BF16),
            pltpu.VMEM((9, 3 * CH, CH), BF16),
            pltpu.VMEM((4, 6, 16, CH), BF16),
            pltpu.VMEM((4, 6, 16, 3 * CH), BF16),
            pltpu.VMEM((32, CH), F32),
            pltpu.VMEM((12, 8, CH), F32),
            pltpu.VMEM((12, 8, CH), F32),
            pltpu.VMEM((4, 32, 384), BF16),
            pltpu.VMEM((GROUPS, 32, 384), BF16),
            pltpu.VMEM((4, 32, 128), BF16),
            pltpu.VMEM((GROUPS, 32, 128), BF16),
            pltpu.VMEM((GROUPS, PART, 32, 128), BF16),
            pltpu.VMEM((GROUPS, PART, 32, 128), BF16),
            pltpu.VMEM((GROUPS, 128, CH), BF16),
            pltpu.VMEM((GROUPS, 16, CH), BF16),
            pltpu.VMEM((256, CH), F32),
            pltpu.VMEM((256, CH), F32),
            pltpu.VMEM((BRICKS, 8, CH), F32),
            pltpu.VMEM((BRICKS, 8, CH), F32),
            pltpu.VMEM((BRICKS, 8, CH), F32),
            pltpu.VMEM((BRICKS, 8, CH), F32),
            pltpu.VMEM((GROUPS, 8, CH), F32),
            pltpu.VMEM((GROUPS, 8, CH), F32),
            pltpu.SemaphoreType.DMA((5,)),
            pltpu.SemaphoreType.DMA((11,)),
            pltpu.SemaphoreType.DMA((11,)),
        ],
        compiler_params=pltpu.CompilerParams(
            collective_id=0, has_side_effects=True, vmem_limit_bytes=32 * 1024 * 1024
        ),
        cost_estimate=pl.CostEstimate(flops=600_000_000, bytes_accessed=2_500_000, transcendentals=40_000),
        name="unet_levels",
    )(field, cotangent, w_fine.reshape(9, 3 * CH, CH), w_coarse.reshape(9, 3 * CH, CH))
    return output, grad_fine.reshape(27, 4, CH), grad_coarse.reshape(27, 4, CH)


def solution(mesh):
    in_specs = (P("group", "brick", None, None), P("group", "brick", None, None), P(), P())
    out_specs = (P("group", "brick", None, None), P(None, "brick", None), P(None, "brick", None))
    return jax.shard_map(body, mesh=mesh, in_specs=in_specs, out_specs=out_specs, check_vma=False)
```

time: 694 us -> 67.4 us (0.10)
  waiting for transfers between devices: 416 us -> 0 us
  blocking collectives: 97.8 us -> 0 us
  Pallas kernels: 0 us -> 60.5 us
  matrix products: 54.2 us -> 0 us
  starting transfers between devices: 52.5 us -> 0 us
  local copies, waits for them, and re-layouts: 50.2 us -> 5.91 us
  between operations: 15.4 us -> 0.65 us
    unnamed x3 -> x0, waiting for transfers between devices: 243 us -> none
    psum x1 -> x0, waiting for transfers between devices: 163 us -> none  [body(): sum_fine, sum_coarse = lax.psum((share_fine, share_coarse), 'group')]
    all_gather x2 -> x0, blocking collectives: 97.8 us -> none  [the longest x1 52.6 us: body(): block = lax.all_gather(coarse, 'brick', axis=1, tiled=True)]
    pallas_call x0 -> x1, Pallas kernels: none -> 60.5 us  [body(): pl.pallas_call(kernel, out_shape=(jax.ShapeDtypeStruct(fine, F32), jax.Sh...]
    dot_general x135 -> x0, matrix products: 54.2 us -> none  [the longest x54 28.8 us: weight_grad(): lax.dot_general(window, flat, (((0,), (0,)), ((), ())), preferred_element...]
    ppermute x8 -> x0, starting transfers between devices: 52.4 us -> none  [the longest x4 43.2 us: extended(): lax.ppermute(tail, axis, [(i, (i + 1) % count) for i in range(ends)])]
    slice x29 -> x0, local copies, waits for them, and re-layouts: 40.5 us -> none  [the longest x28 40.5 us: conv_padded(): padded[step_x:step_x + size_x, step_y:step_y + size_y, step_z:step_z + si...]
    ppermute x8 -> x0, waiting for transfers between devices: 10.7 us -> none  [the longest x4 10.4 us: extended(): lax.ppermute(head, axis, [((i + 1) % count, i) for i in range(ends)])]
  transfers between devices with their start and end apart: 10 -> 0, of which waited for: 6 -> 0; matrix products, arithmetic and copies ran while one was open for 2% -> 0% of each run, Pallas kernels for 0% -> 0%
where the time goes in v1:
time: 67.4 us; the launch traced here: 67.1 us
  Pallas kernels  60.5 us (90%)
  local copies, waits for them, and re-layouts  5.91 us (9%)
    pallas_call x1, Pallas kernels, body(): pl.pallas_call(kernel, out_shape=(jax.ShapeDtypeStruct(fine, F32), jax.Sh...  60.5 us
    unnamed x9, local copies, waits for them, and re-layouts  4.63 us

profile of v1, /device:TPU:1, one launch (start us, length us, event | category | flops | bytes accessed | tf_op | source)
XLA Modules:
  0.0 67.1 jit_solution(3644629997518547372)
XLA Ops:
  0.6 0.0 copy-start
  0.6 1.2 %copy-done = bf16[27,128,128]{2,1,0:T(8,128)(2,1)S(1)} copy-done((bf16[27,128,128]{2,1,0:T(8,128)(2,1)S(1)}, bf16[27,128,128]{2,1,0:T(8,128)(2,1)}, u32[]{:S(2)}) %copy-start) | copy-done | bytes 884760
  1.8 0.0 copy-start.1
  1.8 1.2 %copy-done.1 = bf16[27,128,128]{2,1,0:T(8,128)(2,1)S(1)} copy-done((bf16[27,128,128]{2,1,0:T(8,128)(2,1)S(1)}, bf16[27,128,128]{2,1,0:T(8,128)(2,1)}, u32[]{:S(2)}) %copy-start.1) | copy-done | bytes 884760
  3.0 0.0 copy-start.2
  3.0 0.8 %copy-done.2 = f32[2,4,16,128]{3,2,1,0:T(8,128)S(1)} copy-done((f32[2,4,16,128]{3,2,1,0:T(8,128)S(1)}, f32[2,4,16,128]{3,2,1,0:T(8,128)}, u32[]{:S(2)}) %copy-start.2) | copy-done | bytes 65560
  3.8 0.0 copy-start.3
  3.8 0.8 %copy-done.3 = f32[2,4,16,128]{3,2,1,0:T(8,128)S(1)} copy-done((f32[2,4,16,128]{3,2,1,0:T(8,128)S(1)}, f32[2,4,16,128]{3,2,1,0:T(8,128)}, u32[]{:S(2)}) %copy-start.3) | copy-done | bytes 65560
  4.6 60.5 %unet_levels.1 = (f32[2,4,16,128]{3,2,1,0:T(8,128)S(1)}, f32[108,128]{1,0:T(8,128)S(1)}, f32[108,128]{1,0:T(8,128)S(1)}) custom-call(f32[2,4,16,128]{3,2,1,0:T(8,128)S(1)} %copy-done.2, f32[2,4,16,128]{3,2,1,0:T(8,128)S(1)} %copy-done.3, bf16[9,384,128]{2,1,0:T(8,128)(2,1)S(1)} %bitcast.2, bf16[9,384,128]{2,1,0:T(8,128)(2,1)S(1)} %bitcast.3), custom_call_target="tpu_custom_call" | custom-call | flops 600000000 | bytes 2500000 | tf_op jit(solution)/shard_map/unet_levels/pallas_call | solution.py:315
  65.2 0.6 reshape.20
  65.8 0.6 reshape.21
  66.5 0.6 copy.8
Async XLA Ops:
  0.6 1.2 %copy-start = (bf16[27,128,128]{2,1,0:T(8,128)(2,1)S(1)}, bf16[27,128,128]{2,1,0:T(8,128)(2,1)}, u32[]{:S(2)}) copy-start(bf16[27,128,128]{2,1,0:T(8,128)(2,1)} %param.6) | copy-start | bytes 2654212
  1.8 1.2 %copy-start.1 = (bf16[27,128,128]{2,1,0:T(8,128)(2,1)S(1)}, bf16[27,128,128]{2,1,0:T(8,128)(2,1)}, u32[]{:S(2)}) copy-start(bf16[27,128,128]{2,1,0:T(8,128)(2,1)} %param.7) | copy-start | bytes 2654212
  3.0 0.8 %copy-start.2 = (f32[2,4,16,128]{3,2,1,0:T(8,128)S(1)}, f32[2,4,16,128]{3,2,1,0:T(8,128)}, u32[]{:S(2)}) copy-start(f32[2,4,16,128]{3,2,1,0:T(8,128)} %field.1) | copy-start | bytes 196612
  3.8 0.8 %copy-start.3 = (f32[2,4,16,128]{3,2,1,0:T(8,128)S(1)}, f32[2,4,16,128]{3,2,1,0:T(8,128)}, u32[]{:S(2)}) copy-start(f32[2,4,16,128]{3,2,1,0:T(8,128)} %cot.1) | copy-start | bytes 196612

commit v2 on v1

v2 whole, which is shorter than its diff:
```python
import jax
import jax.numpy as jnp
from jax import lax
from jax.experimental import pallas as pl
from jax.experimental.pallas import tpu as pltpu
from jax.sharding import PartitionSpec as P

CH = 128
GROUPS = 16
BRICKS = 32
F32 = jnp.float32
BF16 = jnp.bfloat16
PART = 7
FAR_FIRST = (10, 11, 6, 7, 14, 15, 8, 9, 2, 3, 12, 13, 4, 5, 1)


def brick_targets(b):
    half, ring = b // 16, b % 16
    steps = sorted(range(16), key=lambda step: -min(step, 16 - step))
    return [
        (flip, step, ((half + flip) % 2) * 16 + (ring + step) % 16)
        for step in steps
        for flip in (1, 0)
        if flip or step
    ]


def wait_for(ref, sem):
    pltpu.make_async_copy(ref, ref, sem).wait()


def iota(shape, dim):
    return lax.broadcasted_iota(jnp.int32, shape, dim)


def neighbours_along_depth(rows, depth):
    count = rows.shape[0]
    place = iota(rows.shape, 0) & (depth - 1)
    before = jnp.where(place == 0, 0.0, pltpu.roll(rows, 1, 0))
    after = jnp.where(place == depth - 1, 0.0, pltpu.roll(rows, count - 1, 0))
    return before, after


def matmul_nt(a, b):
    return lax.dot_general(a, b, (((1,), (1,)), ((), ())), preferred_element_type=F32)


def pooled(values, pool):
    pool[...] = jnp.sum(values.reshape(2, 2, 2, 16, CH), axis=(0, 2)).reshape(32, CH)
    return pool[pl.ds(0, 16, stride=2), :] + pool[pl.ds(1, 16, stride=2), :]


def spread(values, pool):
    pool[pl.ds(0, 16, stride=2), :] = values
    pool[pl.ds(1, 16, stride=2), :] = values
    wide = jnp.broadcast_to(pool[...].reshape(1, 2, 1, 16, CH), (2, 2, 2, 16, CH))
    return wide.reshape(128, CH)


def selection(offset, rows, size_y, size_z):
    row = iota((rows, 128), 0)
    cell = iota((rows, 128), 1)
    step_x, step_y, step_z = offset // 9, (offset // 3) % 3, offset % 3
    plane = size_y * size_z
    z = cell % size_z + step_z - 1
    y = (cell // size_z) % size_y + step_y
    x = cell // plane + step_x
    source = (x * (size_y + 2) + y) * size_z + z
    inside = (z >= 0) & (z < size_z)
    if size_y == 2:
        inside = inside & (cell < plane)
    hit = inside & (row == source) & (offset < 27)
    return jnp.where(hit, 1.0, 0.0).astype(BF16)


def kernel(
    field, cot, w_fine, w_coarse, output, grad_fine, grad_coarse,
    field_v, cot_v, wf_v, wc_v, ext, ext3, pool, cext, gext,
    et_send, et_recv, ct_send, ct_recv, lf, lc, gf, gc, acc_f, acc_c,
    rows, sums, fin,
    local_sem, send_sem, recv_sem, gf_sem,
):
    g = lax.axis_index("group")
    b = lax.axis_index("brick")
    g_up, g_down = (g + 1) % GROUPS, (g + GROUPS - 1) % GROUPS
    b_up, b_down = (b + 1) % BRICKS, (b + BRICKS - 1) % BRICKS
    share, quarter = g // 4, g % 4
    mates = [g + m - 2 * sum(((g // bit) % 2) * bit for bit in (1, 2, 4, 8) if m & bit) for m in range(GROUPS)]

    loads = [
        pltpu.make_async_copy(src, dst, local_sem.at[i])
        for i, (src, dst) in enumerate(((field, field_v), (cot, cot_v), (w_fine, wf_v), (w_coarse, wc_v)))
    ]
    for load in loads:
        load.start()

    barrier = pltpu.get_barrier_semaphore()

    def greet(group, brick):
        pl.semaphore_signal(barrier, inc=1, device_id=(group, brick), device_id_type=pl.DeviceIdType.MESH)

    for brick in brick_targets(b):
        greet(g, brick[2])
    for group in (g_up, g_down):
        for brick in (b_up, b_down):
            greet(group, brick)
    for m in FAR_FIRST:
        greet(mates[m], b)

    def copy_to(src, dst, send, recv, group, brick):
        return pltpu.make_async_remote_copy(
            src_ref=src,
            dst_ref=dst,
            send_sem=send,
            recv_sem=recv,
            device_id=(group, brick),
            device_id_type=pl.DeviceIdType.MESH,
        )

    def send(src, dst, phase, group, brick):
        copy_to(src, dst, send_sem.at[phase], recv_sem.at[phase], group, brick).start()

    arrivals = (
        ext.at[pl.ds(0, 4), pl.ds(0, 4)],
        et_recv.at[pl.ds(0, 7), 0],
        cext.at[pl.ds(0, 10)],
        gext.at[pl.ds(0, 10)],
        gc.at[pl.ds(0, GROUPS - 1)],
        ct_recv.at[pl.ds(0, GROUPS - 1)],
        et_recv.at[pl.ds(0, 8), 0],
        sums.at[pl.ds(0, BRICKS - 1)],
        fin.at[pl.ds(0, GROUPS - 1)],
    )

    def arrived(phase):
        wait_for(arrivals[phase], recv_sem.at[phase])

    def sent(phase):
        wait_for(arrivals[phase], send_sem.at[phase])

    loads[0].wait()
    ext[1:3, 1:5] = field_v[...].astype(BF16)
    pl.semaphore_wait(barrier, 4 + GROUPS - 1 + BRICKS - 1)

    send(ext.at[1, 1], ext.at[3, 5], 0, g_down, b_down)
    send(ext.at[1, 4], ext.at[3, 0], 0, g_down, b_up)
    send(ext.at[2, 1], ext.at[0, 5], 0, g_up, b_down)
    send(ext.at[2, 4], ext.at[0, 0], 0, g_up, b_up)
    send(ext.at[1, pl.ds(1, 4)], ext.at[3, pl.ds(1, 4)], 0, g_down, b)
    send(ext.at[2, pl.ds(1, 4)], ext.at[0, pl.ds(1, 4)], 0, g_up, b)
    send(ext.at[pl.ds(1, 2), 1], ext.at[pl.ds(1, 2), 5], 0, g, b_down)
    send(ext.at[pl.ds(1, 2), 4], ext.at[pl.ds(1, 2), 0], 0, g, b_up)

    loads[1].wait()
    d_coarse = pooled(cot_v[...].reshape(128, CH), pool)
    order = iota((CH, CH), 0)
    sort = jnp.where(iota((CH, CH), 1) == 4 * (order % 32) + order // 32, 1.0, 0.0).astype(BF16)
    loads[2].wait()
    loads[3].wait()

    arrived(0)

    def clear(outside, part):
        @pl.when(outside)
        def _():
            ext[part] = jnp.zeros(ext.at[part].shape, BF16)

    clear(g == 0, slice(0, 1))
    clear(g == GROUPS - 1, slice(3, 4))
    clear(b == 0, (slice(0, 4), slice(0, 1)))
    clear(b == BRICKS - 1, (slice(0, 4), slice(5, 6)))

    cells = ext[...].reshape(384, CH)
    before, after = neighbours_along_depth(cells.astype(F32), 16)
    ext3[:, :, :, 0:CH] = before.astype(BF16).reshape(4, 6, 16, CH)
    ext3[:, :, :, CH : 2 * CH] = ext[...]
    ext3[:, :, :, 2 * CH :] = after.astype(BF16).reshape(4, 6, 16, CH)

    z_fine = jnp.zeros((128, CH), F32)
    for step in range(9):
        step_x, step_y = step // 3, step % 3
        window = ext3[step_x : step_x + 2, step_y : step_y + 4].reshape(128, 3 * CH)
        z_fine = z_fine + jnp.dot(window, wf_v[step], preferred_element_type=F32)
    sig = jax.nn.sigmoid(z_fine)
    act_fine = z_fine * sig
    slope_fine = sig * (1.0 + z_fine * (1.0 - sig))
    coarse = (pooled(act_fine, pool) * 0.125).astype(BF16).astype(F32)

    def coarse_halo(buf, phase):
        send(buf.at[5], buf.at[11], phase, g_down, b_down)
        send(buf.at[6], buf.at[8], phase, g_down, b_up)
        send(buf.at[5], buf.at[3], phase, g_up, b_down)
        send(buf.at[6], buf.at[0], phase, g_up, b_up)
        send(buf.at[pl.ds(5, 2)], buf.at[pl.ds(9, 2)], phase, g_down, b)
        send(buf.at[pl.ds(5, 2)], buf.at[pl.ds(1, 2)], phase, g_up, b)
        send(buf.at[5], buf.at[7], phase, g, b_down)
        send(buf.at[6], buf.at[4], phase, g, b_up)

    def coarse_halo_wait(buf, phase):
        arrived(phase)

        def clear(outside, rows):
            @pl.when(outside)
            def _():
                for row in rows:
                    buf[row] = jnp.zeros((8, CH), F32)

        clear(g == 0, (0, 1, 2, 3))
        clear(g == GROUPS - 1, (8, 9, 10, 11))
        clear(b == 0, (0, 4, 8))
        clear(b == BRICKS - 1, (3, 7, 11))

    cext[5:7] = coarse.reshape(2, 8, CH)
    coarse_halo(cext, 2)

    et_send[...] = matmul_nt(sort, cells).astype(BF16).reshape(4, 32, 384)
    for m in FAR_FIRST:
        if m % 2 == 0:
            send(et_send.at[mates[m] // 4], et_recv.at[m // 2, 0], 1, mates[m], b)
    send(et_send.at[share], et_recv.at[0, 1], 6, mates[1], b)
    et_recv[0, 0] = et_send[share]

    coarse_halo_wait(cext, 2)

    ccells = cext[...].reshape(96, CH)
    before, after = neighbours_along_depth(ccells, 8)
    wide = jnp.concatenate([before, ccells, after], axis=1)
    z_coarse = jnp.zeros((16, CH), F32)
    for step in range(9):
        start = (step // 3) * 32 + (step % 3) * 8
        window = wide[start : start + 16].astype(BF16)
        z_coarse = z_coarse + jnp.dot(window, wc_v[step], preferred_element_type=F32)
    sig = jax.nn.sigmoid(z_coarse)
    act_coarse = z_coarse * sig
    g_coarse = d_coarse * (sig * (1.0 + z_coarse * (1.0 - sig)))
    g_coarse = g_coarse.astype(BF16)
    gext[5:7] = g_coarse.astype(F32).reshape(2, 8, CH)
    coarse_halo(gext, 3)

    gc[0] = g_coarse
    for m in FAR_FIRST:
        send(gc.at[0], gc.at[m], 4, mates[m], b)
    ccells = jnp.concatenate([ccells, jnp.zeros((32, CH), F32)], axis=0).astype(BF16)
    ct_send[...] = matmul_nt(sort, ccells).astype(BF16).reshape(4, 32, 128)
    for m in FAR_FIRST:
        send(ct_send.at[mates[m] // 4], ct_recv.at[m], 5, mates[m], b)
    ct_recv[0] = ct_send[share]

    output[...] = (act_fine + spread(act_coarse, pool)).reshape(2, 4, 16, CH)

    arrived(1)
    send(et_recv.at[pl.ds(1, 7), 0], et_recv.at[pl.ds(1, 7), 1], 6, mates[1], b)

    coarse_halo_wait(gext, 3)
    gcells = gext[...].reshape(96, CH)
    mixed = jnp.zeros((16, 3 * CH), F32)
    for step in range(9):
        start = (2 - step // 3) * 32 + (2 - step % 3) * 8
        window = gcells[start : start + 16].astype(BF16)
        mixed = mixed + matmul_nt(window, wc_v[step])
    back_coarse = mixed[:, CH : 2 * CH]
    back_coarse = back_coarse + neighbours_along_depth(mixed[:, 0:CH], 8)[1]
    back_coarse = back_coarse + neighbours_along_depth(mixed[:, 2 * CH :], 8)[0]
    g_fine = (cot_v[...].reshape(128, CH) + spread(back_coarse, pool) * 0.125) * slope_fine
    gf[0] = g_fine.astype(BF16)

    def gf_copy(src, dst, m):
        return copy_to(gf.at[src], gf.at[dst], gf_sem.at[GROUPS + dst], gf_sem.at[dst], mates[m], b)

    for m in FAR_FIRST:
        if m % 2 == 0:
            gf_copy(0, m, m).start()
    gf_copy(0, 1, 1).start()

    arrived(6)
    everyone = et_recv[...].reshape(GROUPS * 32, 384)
    for k in range(PART):
        picked = jnp.dot(everyone, selection(quarter * PART + k, 384, 4, 16), preferred_element_type=F32)
        lf[:, k] = picked.astype(BF16).reshape(GROUPS, 32, 128)
    arrived(5)
    everyone = ct_recv[...].reshape(GROUPS * 32, 128)
    for k in range(PART):
        picked = jnp.dot(everyone, selection(quarter * PART + k, 128, 2, 8), preferred_element_type=F32)
        lc[:, k] = picked.astype(BF16).reshape(GROUPS, 32, 128)

    arrived(4)
    total = jnp.zeros((PART * 32, CH), F32)
    for m in range(GROUPS):
        grads = jnp.concatenate([gc[m], jnp.zeros((112, CH), BF16)], axis=0)
        total = total + jnp.dot(lc[m].reshape(PART * 32, 128), grads, preferred_element_type=F32)
    acc_c[0 : PART * 32] = total
    acc_c[PART * 32 :] = jnp.zeros((32, CH), F32)
    acc_f[PART * 32 :] = jnp.zeros((32, CH), F32)

    total = jnp.dot(lf[0].reshape(PART * 32, 128), gf[0], preferred_element_type=F32)

    def take(total, m):
        gf_copy(0, m, m).wait_recv()
        if m % 2 == 0:
            gf_copy(m, m + 1, 1).start()
        return total + jnp.dot(lf[m].reshape(PART * 32, 128), gf[m], preferred_element_type=F32)

    last = 1
    for m in reversed(FAR_FIRST):
        if m % 2 == 0:
            total = take(total, m)
            total = take(total, last)
            last = m + 1
    total = take(total, last)

    acc_f[0 : PART * 32] = total
    for brick in range(BRICKS):
        pair = [acc[pl.ds(brick, 8, stride=32), :] for acc in (acc_f, acc_c)]
        rows[brick] = jnp.concatenate(pair, axis=0).astype(BF16)
    for high, step, brick in brick_targets(b):
        send(rows.at[brick], sums.at[high * 16 + step], 7, g, brick)
    sums[0] = rows[b]
    arrived(7)
    fin[g] = jnp.sum(sums[...].astype(F32), axis=0)
    for m in FAR_FIRST:
        send(fin.at[g], fin.at[g], 8, mates[m], b)

    for phase in range(8):
        sent(phase)
    for m in range(1, GROUPS):
        gf_copy(0, m, m).wait_send()

    arrived(8)
    for member in range(GROUPS):
        channel, part = member // 4, member % 4
        count = PART if part < 3 else PART - 1
        where = pl.ds(part * PART, count)
        grad_fine[where, channel, :] = fin[member, 0:count]
        grad_coarse[where, channel, :] = fin[member, 8 : 8 + count]
    sent(8)


def copy_out(output, grad_fine, grad_coarse, output_to, grad_fine_to, grad_coarse_to, sem):
    copies = [
        pltpu.make_async_copy(src, dst, sem.at[i])
        for i, (src, dst) in enumerate(
            ((output, output_to), (grad_fine, grad_fine_to), (grad_coarse, grad_coarse_to))
        )
    ]
    for copy in copies:
        copy.start()
    for copy in copies:
        copy.wait()


def body(field, cotangent, w_fine, w_coarse):
    anywhere = pl.BlockSpec(memory_space=pl.ANY)
    vmem = pl.BlockSpec(memory_space=pltpu.VMEM)
    fine = (2, 4, 16, CH)
    shapes = (
        jax.ShapeDtypeStruct(fine, F32),
        jax.ShapeDtypeStruct((27, 4, CH), F32),
        jax.ShapeDtypeStruct((27, 4, CH), F32),
    )
    results = pl.pallas_call(
        kernel,
        out_shape=tuple(pltpu.VMEM(shape.shape, shape.dtype) for shape in shapes),
        in_specs=[anywhere] * 4,
        out_specs=(vmem, vmem, vmem),
        scratch_shapes=[
            pltpu.VMEM(fine, F32),
            pltpu.VMEM(fine, F32),
            pltpu.VMEM((9, 3 * CH, CH), BF16),
            pltpu.VMEM((9, 3 * CH, CH), BF16),
            pltpu.VMEM((4, 6, 16, CH), BF16),
            pltpu.VMEM((4, 6, 16, 3 * CH), BF16),
            pltpu.VMEM((32, CH), F32),
            pltpu.VMEM((12, 8, CH), F32),
            pltpu.VMEM((12, 8, CH), F32),
            pltpu.VMEM((4, 32, 384), BF16),
            pltpu.VMEM((8, 2, 32, 384), BF16),
            pltpu.VMEM((4, 32, 128), BF16),
            pltpu.VMEM((GROUPS, 32, 128), BF16),
            pltpu.VMEM((GROUPS, PART, 32, 128), BF16),
            pltpu.VMEM((GROUPS, PART, 32, 128), BF16),
            pltpu.VMEM((GROUPS, 128, CH), BF16),
            pltpu.VMEM((GROUPS, 16, CH), BF16),
            pltpu.VMEM((256, CH), F32),
            pltpu.VMEM((256, CH), F32),
            pltpu.VMEM((BRICKS, 16, CH), BF16),
            pltpu.VMEM((BRICKS, 16, CH), BF16),
            pltpu.VMEM((GROUPS, 16, CH), F32),
            pltpu.SemaphoreType.DMA((4,)),
            pltpu.SemaphoreType.DMA((9,)),
            pltpu.SemaphoreType.DMA((9,)),
            pltpu.SemaphoreType.DMA((2 * GROUPS,)),
        ],
        compiler_params=pltpu.CompilerParams(
            collective_id=0, has_side_effects=True, vmem_limit_bytes=60 * 1024 * 1024
        ),
        cost_estimate=pl.CostEstimate(flops=600_000_000, bytes_accessed=2_500_000, transcendentals=40_000),
        name="unet_levels",
    )(field, cotangent, w_fine.reshape(9, 3 * CH, CH), w_coarse.reshape(9, 3 * CH, CH))
    return pl.pallas_call(
        copy_out,
        out_shape=shapes,
        in_specs=[vmem] * 3,
        out_specs=(anywhere,) * 3,
        scratch_shapes=[pltpu.SemaphoreType.DMA((3,))],
        compiler_params=pltpu.CompilerParams(vmem_limit_bytes=1024 * 1024),
        name="copy_out",
    )(*results)


def solution(mesh):
    in_specs = (P("group", "brick", None, None), P("group", "brick", None, None), P(), P())
    out_specs = (P("group", "brick", None, None), P(None, "brick", None), P(None, "brick", None))
    return jax.shard_map(body, mesh=mesh, in_specs=in_specs, out_specs=out_specs, check_vma=False)
```

time: 67.4 us -> 56.6 us (0.84)
  local copies, waits for them, and re-layouts: 5.91 us -> 0 us
  Pallas kernels: 60.5 us -> 55.8 us
    pallas_call x1 -> x2, Pallas kernels: 60.5 us -> 55.8 us  [the longest x1 55.1 us: body(): pl.pallas_call(kernel, out_shape=tuple((pltpu.VMEM(shape.shape, shape.dty...]
    unnamed x9 -> x0, local copies, waits for them, and re-layouts: 4.63 us -> none
    reshape x2 -> x0, local copies, waits for them, and re-layouts: 1.28 us -> none  [the longest x1 0.64 us: body(): grad_fine.reshape(27, 4, CH)]
where the time goes in v2:
time: 56.6 us; the launch traced here: 56.4 us
  Pallas kernels  55.8 us (99%)
  between operations  0.64 us (1%)
    pallas_call x1, Pallas kernels, body(): pl.pallas_call(kernel, out_shape=tuple((pltpu.VMEM(shape.shape, shape.dty...  55.1 us

profile of v2, /device:TPU:1, one launch (start us, length us, event | category | flops | bytes accessed | tf_op | source)
XLA Modules:
  0.0 56.4 jit_solution(13348415578777827523)
XLA Ops:
  0.6 55.1 %unet_levels.1 = (f32[2,4,16,128]{3,2,1,0:T(8,128)S(1)}, f32[27,4,128]{2,1,0:T(4,128)S(1)}, f32[27,4,128]{2,1,0:T(4,128)S(1)}) custom-call(f32[2,4,16,128]{3,2,1,0:T(8,128)} %field.1, f32[2,4,16,128]{3,2,1,0:T(8,128)} %cot.1, bf16[9,384,128]{2,1,0:T(8,128)(2,1)} %bitcast.2, bf16[9,384,128]{2,1,0:T(8,128)(2,1)} %bitcast.3), custom_call_target="tpu_custom_call" | custom-call | flops 600000000 | bytes 2500000 | tf_op jit(solution)/shard_map/unet_levels/pallas_call | solution.py:360
  55.7 0.7 %copy_out.1 = (f32[2,4,16,128]{3,2,1,0:T(8,128)}, f32[27,4,128]{2,1,0:T(4,128)}, f32[27,4,128]{2,1,0:T(4,128)}) custom-call(f32[2,4,16,128]{3,2,1,0:T(8,128)S(1)} %get-tuple-element.6.output, f32[27,4,128]{2,1,0:T(4,128)S(1)} %get-tuple-element.7.grad_fine, f32[27,4,128]{2,1,0:T(4,128)S(1)} %get-tuple-element.8.grad_coarse), custom_call_target="tpu_custom_call" | custom-call | tf_op jit(solution)/shard_map/copy_out/pallas_call | solution.py:399

commit v3 on v2

--- a/solution.py
+++ b/solution.py
@@ -75,10 +75,10 @@
 
 def kernel(
     field, cot, w_fine, w_coarse, output, grad_fine, grad_coarse,
-    field_v, cot_v, wf_v, wc_v, ext, ext3, pool, cext, gext,
-    et_send, et_recv, ct_send, ct_recv, lf, lc, gf, gc, acc_f, acc_c,
+    field_v, cot_v, wf_v, wc_v, ext, ext3, pool, wide_pool, cext, gext,
+    et_send, et_all, cot_all, slope_all, ct_send, ct_all, lf, lc, acc_f, acc_c,
     rows, sums, fin,
-    local_sem, send_sem, recv_sem, gf_sem,
+    local_sem, send_sem, recv_sem,
 ):
     g = lax.axis_index("group")
     b = lax.axis_index("brick")
@@ -122,14 +122,17 @@
 
     arrivals = (
         ext.at[pl.ds(0, 4), pl.ds(0, 4)],
-        et_recv.at[pl.ds(0, 7), 0],
+        cot_all.at[pl.ds(0, 7), 0],
         cext.at[pl.ds(0, 10)],
-        gext.at[pl.ds(0, 10)],
-        gc.at[pl.ds(0, GROUPS - 1)],
-        ct_recv.at[pl.ds(0, GROUPS - 1)],
-        et_recv.at[pl.ds(0, 8), 0],
+        slope_all.at[pl.ds(0, 7), 0],
+        gext.at[pl.ds(0, 3 * GROUPS - 1)],
+        ct_all.at[pl.ds(0, GROUPS - 1)],
+        et_all.at[pl.ds(0, 7), 0],
         sums.at[pl.ds(0, BRICKS - 1)],
         fin.at[pl.ds(0, GROUPS - 1)],
+        cot_all.at[pl.ds(0, 8), 0],
+        slope_all.at[pl.ds(0, 8), 0],
+        et_all.at[pl.ds(0, 8), 0],
     )
 
     def arrived(phase):
@@ -137,6 +140,17 @@
 
     def sent(phase):
         wait_for(arrivals[phase], send_sem.at[phase])
+
+    chip, core = g // 2, g % 2
+
+    def spread_out(src_of, buf, phase):
+        for m in FAR_FIRST:
+            if m % 2 == 0:
+                send(src_of(mates[m]), buf.at[chip, core], phase, mates[m], b)
+
+    def relay(buf, phase, after):
+        arrived(phase)
+        send(buf.at[:, core], buf.at[:, core], after, mates[1], b)
 
     loads[0].wait()
     ext[1:3, 1:5] = field_v[...].astype(BF16)
@@ -152,7 +166,10 @@
     send(ext.at[pl.ds(1, 2), 4], ext.at[pl.ds(1, 2), 0], 0, g, b_up)
 
     loads[1].wait()
-    d_coarse = pooled(cot_v[...].reshape(128, CH), pool)
+    cot_rows = cot_v[...].reshape(128, CH)
+    cot_all[chip, core] = cot_rows.astype(BF16)
+    spread_out(lambda mate: cot_all.at[chip, core], cot_all, 1)
+    d_coarse = pooled(cot_rows, pool)
     order = iota((CH, CH), 0)
     sort = jnp.where(iota((CH, CH), 1) == 4 * (order % 32) + order // 32, 1.0, 0.0).astype(BF16)
     loads[2].wait()
@@ -213,12 +230,13 @@
     cext[5:7] = coarse.reshape(2, 8, CH)
     coarse_halo(cext, 2)
 
+    slope_all[chip, core] = slope_fine.astype(BF16)
+    spread_out(lambda mate: slope_all.at[chip, core], slope_all, 3)
+
     et_send[...] = matmul_nt(sort, cells).astype(BF16).reshape(4, 32, 384)
-    for m in FAR_FIRST:
-        if m % 2 == 0:
-            send(et_send.at[mates[m] // 4], et_recv.at[m // 2, 0], 1, mates[m], b)
-    send(et_send.at[share], et_recv.at[0, 1], 6, mates[1], b)
-    et_recv[0, 0] = et_send[share]
+    spread_out(lambda mate: et_send.at[mate // 4], et_all, 6)
+    et_all[chip, core] = et_send[share]
+    relay(cot_all, 1, 9)
 
     coarse_halo_wait(cext, 2)
 
@@ -234,81 +252,93 @@
     act_coarse = z_coarse * sig
     g_coarse = d_coarse * (sig * (1.0 + z_coarse * (1.0 - sig)))
     g_coarse = g_coarse.astype(BF16)
-    gext[5:7] = g_coarse.astype(F32).reshape(2, 8, CH)
-    coarse_halo(gext, 3)
-
-    gc[0] = g_coarse
-    for m in FAR_FIRST:
-        send(gc.at[0], gc.at[m], 4, mates[m], b)
+
+    own = (g + 1) * 3
+    gext[own + 1] = g_coarse
+    for m in FAR_FIRST + (0,):
+        send(gext.at[own + 1], gext.at[own + 2], 4, mates[m], b_down)
+        send(gext.at[own + 1], gext.at[own], 4, mates[m], b_up)
+        if m:
+            send(gext.at[own + 1], gext.at[own + 1], 4, mates[m], b)
+    for row in (0, 1, 2, 51, 52, 53):
+        gext[row] = jnp.zeros((16, CH), BF16)
+
     ccells = jnp.concatenate([ccells, jnp.zeros((32, CH), F32)], axis=0).astype(BF16)
     ct_send[...] = matmul_nt(sort, ccells).astype(BF16).reshape(4, 32, 128)
     for m in FAR_FIRST:
-        send(ct_send.at[mates[m] // 4], ct_recv.at[m], 5, mates[m], b)
-    ct_recv[0] = ct_send[share]
+        send(ct_send.at[mates[m] // 4], ct_all.at[g], 5, mates[m], b)
+    ct_all[g] = ct_send[share]
 
     output[...] = (act_fine + spread(act_coarse, pool)).reshape(2, 4, 16, CH)
 
-    arrived(1)
-    send(et_recv.at[pl.ds(1, 7), 0], et_recv.at[pl.ds(1, 7), 1], 6, mates[1], b)
-
-    coarse_halo_wait(gext, 3)
-    gcells = gext[...].reshape(96, CH)
-    mixed = jnp.zeros((16, 3 * CH), F32)
+    relay(slope_all, 3, 10)
+    relay(et_all, 6, 11)
+
+    arrived(11)
+    everyone = et_all[...].reshape(GROUPS * 32, 384)
+    for k in range(0, PART, 2):
+        steps = range(k, min(k + 2, PART))
+        chosen = [selection(quarter * PART + step, 384, 4, 16) for step in steps]
+        picked = jnp.dot(everyone, jnp.concatenate(chosen, axis=1), preferred_element_type=F32)
+        picked = picked.astype(BF16).reshape(8, 2, 32, len(chosen) * 128)
+        for i, step in enumerate(steps):
+            for half in range(2):
+                lf[:, step, :, half * 128 : (half + 1) * 128] = picked[:, half, :, i * 128 : (i + 1) * 128]
+    arrived(5)
+    everyone = ct_all[...].reshape(GROUPS * 32, 128)
+    for k in range(0, PART, 2):
+        steps = range(k, min(k + 2, PART))
+        chosen = [selection(quarter * PART + step, 128, 2, 8) for step in steps]
+        picked = jnp.dot(everyone, jnp.concatenate(chosen, axis=1), preferred_element_type=F32)
+        picked = picked.astype(BF16).reshape(8, 2, 32, len(chosen) * 128)
+        for i, step in enumerate(steps):
+            for half in range(2):
+                lc[:, step, :, half * 128 : (half + 1) * 128] = picked[:, half, :, i * 128 : (i + 1) * 128]
+    arrived(9)
+    arrived(10)
+
+    arrived(4)
+
+    def clear_gext(outside, place):
+        @pl.when(outside)
+        def _():
+            for x in range(GROUPS):
+                gext[(x + 1) * 3 + place] = jnp.zeros((16, CH), BF16)
+
+    clear_gext(b == 0, 0)
+    clear_gext(b == BRICKS - 1, 2)
+
+    gcells = gext[...].astype(F32).reshape(GROUPS + 2, 6, 8, CH)
+    mixed = jnp.zeros((GROUPS * 16, 3 * CH), F32)
     for step in range(9):
-        start = (2 - step // 3) * 32 + (2 - step % 3) * 8
-        window = gcells[start : start + 16].astype(BF16)
-        mixed = mixed + matmul_nt(window, wc_v[step])
+        step_x, step_y = step // 3, step % 3
+        window = gcells[2 - step_x : 18 - step_x, 3 - step_y : 5 - step_y].reshape(GROUPS * 16, CH)
+        mixed = mixed + matmul_nt(window.astype(BF16), wc_v[step])
     back_coarse = mixed[:, CH : 2 * CH]
     back_coarse = back_coarse + neighbours_along_depth(mixed[:, 0:CH], 8)[1]
     back_coarse = back_coarse + neighbours_along_depth(mixed[:, 2 * CH :], 8)[0]
-    g_fine = (cot_v[...].reshape(128, CH) + spread(back_coarse, pool) * 0.125) * slope_fine
-    gf[0] = g_fine.astype(BF16)
-
-    def gf_copy(src, dst, m):
-        return copy_to(gf.at[src], gf.at[dst], gf_sem.at[GROUPS + dst], gf_sem.at[dst], mates[m], b)
-
-    for m in FAR_FIRST:
-        if m % 2 == 0:
-            gf_copy(0, m, m).start()
-    gf_copy(0, 1, 1).start()
-
-    arrived(6)
-    everyone = et_recv[...].reshape(GROUPS * 32, 384)
-    for k in range(PART):
-        picked = jnp.dot(everyone, selection(quarter * PART + k, 384, 4, 16), preferred_element_type=F32)
-        lf[:, k] = picked.astype(BF16).reshape(GROUPS, 32, 128)
-    arrived(5)
-    everyone = ct_recv[...].reshape(GROUPS * 32, 128)
-    for k in range(PART):
-        picked = jnp.dot(everyone, selection(quarter * PART + k, 128, 2, 8), preferred_element_type=F32)
-        lc[:, k] = picked.astype(BF16).reshape(GROUPS, 32, 128)
-
-    arrived(4)
+    back_coarse = back_coarse * 0.125
+    wide_pool[pl.ds(0, GROUPS * 16, stride=2), :] = back_coarse
+    wide_pool[pl.ds(1, GROUPS * 16, stride=2), :] = back_coarse
     total = jnp.zeros((PART * 32, CH), F32)
-    for m in range(GROUPS):
-        grads = jnp.concatenate([gc[m], jnp.zeros((112, CH), BF16)], axis=0)
-        total = total + jnp.dot(lc[m].reshape(PART * 32, 128), grads, preferred_element_type=F32)
+    for pair in range(8):
+        back = wide_pool[pair * 64 : (pair + 1) * 64].reshape(2, 1, 2, 1, 16, CH)
+        back = jnp.broadcast_to(back, (2, 2, 2, 2, 16, CH)).reshape(256, CH)
+        grads = cot_all[pair].reshape(256, CH).astype(F32) + back
+        grads = (grads * slope_all[pair].reshape(256, CH).astype(F32)).astype(BF16)
+        total = total + jnp.dot(lf[pair].reshape(PART * 32, 256), grads, preferred_element_type=F32)
+    acc_f[0 : PART * 32] = total
+
+    total = jnp.zeros((PART * 32, CH), F32)
+    empty = jnp.zeros((112, CH), BF16)
+    for pair in range(8):
+        first, second = (gext[(2 * pair + i + 1) * 3 + 1] for i in range(2))
+        grads = jnp.concatenate([first, empty, second, empty], axis=0)
+        total = total + jnp.dot(lc[pair].reshape(PART * 32, 256), grads, preferred_element_type=F32)
     acc_c[0 : PART * 32] = total
     acc_c[PART * 32 :] = jnp.zeros((32, CH), F32)
     acc_f[PART * 32 :] = jnp.zeros((32, CH), F32)
 
-    total = jnp.dot(lf[0].reshape(PART * 32, 128), gf[0], preferred_element_type=F32)
-
-    def take(total, m):
-        gf_copy(0, m, m).wait_recv()
-        if m % 2 == 0:
-            gf_copy(m, m + 1, 1).start()
-        return total + jnp.dot(lf[m].reshape(PART * 32, 128), gf[m], preferred_element_type=F32)
-
-    last = 1
-    for m in reversed(FAR_FIRST):
-        if m % 2 == 0:
-            total = take(total, m)
-            total = take(total, last)
-            last = m + 1
-    total = take(total, last)
-
-    acc_f[0 : PART * 32] = total
     for brick in range(BRICKS):
         pair = [acc[pl.ds(brick, 8, stride=32), :] for acc in (acc_f, acc_c)]
         rows[brick] = jnp.concatenate(pair, axis=0).astype(BF16)
@@ -320,10 +350,8 @@
     for m in FAR_FIRST:
         send(fin.at[g], fin.at[g], 8, mates[m], b)
 
-    for phase in range(8):
+    for phase in (0, 1, 2, 3, 4, 5, 6, 7, 9, 10, 11):
         sent(phase)
-    for m in range(1, GROUPS):
-        gf_copy(0, m, m).wait_send()
 
     arrived(8)
     for member in range(GROUPS):
@@ -370,25 +398,25 @@
             pltpu.VMEM((4, 6, 16, CH), BF16),
             pltpu.VMEM((4, 6, 16, 3 * CH), BF16),
             pltpu.VMEM((32, CH), F32),
+            pltpu.VMEM((GROUPS * 32, CH), F32),
             pltpu.VMEM((12, 8, CH), F32),
-            pltpu.VMEM((12, 8, CH), F32),
+            pltpu.VMEM(((GROUPS + 2) * 3, 16, CH), BF16),
             pltpu.VMEM((4, 32, 384), BF16),
             pltpu.VMEM((8, 2, 32, 384), BF16),
+            pltpu.VMEM((8, 2, 128, CH), BF16),
+            pltpu.VMEM((8, 2, 128, CH), BF16),
             pltpu.VMEM((4, 32, 128), BF16),
             pltpu.VMEM((GROUPS, 32, 128), BF16),
-            pltpu.VMEM((GROUPS, PART, 32, 128), BF16),
-            pltpu.VMEM((GROUPS, PART, 32, 128), BF16),
-            pltpu.VMEM((GROUPS, 128, CH), BF16),
-            pltpu.VMEM((GROUPS, 16, CH), BF16),
+            pltpu.VMEM((8, PART, 32, 256), BF16),
+            pltpu.VMEM((8, PART, 32, 256), BF16),
             pltpu.VMEM((256, CH), F32),
             pltpu.VMEM((256, CH), F32),
             pltpu.VMEM((BRICKS, 16, CH), BF16),
             pltpu.VMEM((BRICKS, 16, CH), BF16),
             pltpu.VMEM((GROUPS, 16, CH), F32),
             pltpu.SemaphoreType.DMA((4,)),
-            pltpu.SemaphoreType.DMA((9,)),
-            pltpu.SemaphoreType.DMA((9,)),
-            pltpu.SemaphoreType.DMA((2 * GROUPS,)),
+            pltpu.SemaphoreType.DMA((12,)),
+            pltpu.SemaphoreType.DMA((12,)),
         ],
         compiler_params=pltpu.CompilerParams(
             collective_id=0, has_side_effects=True, vmem_limit_bytes=60 * 1024 * 1024

time: 56.6 us -> 52.4 us (0.926)
  Pallas kernels: 55.8 us -> 51.6 us
    pallas_call x1, Pallas kernels: 55.1 us -> 50.9 us  [body(): pl.pallas_call(kernel, out_shape=tuple((pltpu.VMEM(shape.shape, shape.dty...]
where the time goes in v3:
time: 52.4 us; the launch traced here: 52.2 us
  Pallas kernels  51.6 us (98%)
  between operations  0.64 us (1%)
    pallas_call x1, Pallas kernels, body(): pl.pallas_call(kernel, out_shape=tuple((pltpu.VMEM(shape.shape, shape.dty...  50.9 us

profile of v3, /device:TPU:1, one launch (start us, length us, event | category | flops | bytes accessed | tf_op | source)
XLA Modules:
  0.0 52.2 jit_solution(8831760662815635469)
XLA Ops:
  0.6 50.9 %unet_levels.1 = (f32[2,4,16,128]{3,2,1,0:T(8,128)S(1)}, f32[27,4,128]{2,1,0:T(4,128)S(1)}, f32[27,4,128]{2,1,0:T(4,128)S(1)}) custom-call(f32[2,4,16,128]{3,2,1,0:T(8,128)} %field.1, f32[2,4,16,128]{3,2,1,0:T(8,128)} %cot.1, bf16[9,384,128]{2,1,0:T(8,128)(2,1)} %bitcast.2, bf16[9,384,128]{2,1,0:T(8,128)(2,1)} %bitcast.3), custom_call_target="tpu_custom_call" | custom-call | flops 600000000 | bytes 2500000 | tf_op jit(solution)/shard_map/unet_levels/pallas_call | solution.py:388
  51.5 0.7 %copy_out.1 = (f32[2,4,16,128]{3,2,1,0:T(8,128)}, f32[27,4,128]{2,1,0:T(4,128)}, f32[27,4,128]{2,1,0:T(4,128)}) custom-call(f32[2,4,16,128]{3,2,1,0:T(8,128)S(1)} %get-tuple-element.6.output, f32[27,4,128]{2,1,0:T(4,128)S(1)} %get-tuple-element.7.grad_fine, f32[27,4,128]{2,1,0:T(4,128)S(1)} %get-tuple-element.8.grad_coarse), custom_call_target="tpu_custom_call" | custom-call | tf_op jit(solution)/shard_map/copy_out/pallas_call | solution.py:427

commit v4 on v3

--- a/solution.py
+++ b/solution.py
@@ -78,7 +78,7 @@
     field_v, cot_v, wf_v, wc_v, ext, ext3, pool, wide_pool, cext, gext,
     et_send, et_all, cot_all, slope_all, ct_send, ct_all, lf, lc, acc_f, acc_c,
     rows, sums, fin,
-    local_sem, send_sem, recv_sem,
+    local_sem, send_sem, recv_sem, ring_sem,
 ):
     g = lax.axis_index("group")
     b = lax.axis_index("brick")
@@ -99,13 +99,22 @@
     def greet(group, brick):
         pl.semaphore_signal(barrier, inc=1, device_id=(group, brick), device_id_type=pl.DeviceIdType.MESH)
 
-    for brick in brick_targets(b):
-        greet(g, brick[2])
     for group in (g_up, g_down):
         for brick in (b_up, b_down):
             greet(group, brick)
     for m in FAR_FIRST:
         greet(mates[m], b)
+    greet(g, b_up)
+    greet(g, b_down)
+
+    def tell(stage):
+        for brick in ((b + 2**stage) % BRICKS, (b + BRICKS - 2**stage) % BRICKS):
+            pl.semaphore_signal(
+                ring_sem.at[stage], inc=1, device_id=(g, brick), device_id_type=pl.DeviceIdType.MESH
+            )
+
+    def heard(stage):
+        pl.semaphore_wait(ring_sem.at[stage], 2)
 
     def copy_to(src, dst, send, recv, group, brick):
         return pltpu.make_async_remote_copy(
@@ -154,7 +163,7 @@
 
     loads[0].wait()
     ext[1:3, 1:5] = field_v[...].astype(BF16)
-    pl.semaphore_wait(barrier, 4 + GROUPS - 1 + BRICKS - 1)
+    pl.semaphore_wait(barrier, 6 + GROUPS - 1)
 
     send(ext.at[1, 1], ext.at[3, 5], 0, g_down, b_down)
     send(ext.at[1, 4], ext.at[3, 0], 0, g_down, b_up)
@@ -164,6 +173,8 @@
     send(ext.at[2, pl.ds(1, 4)], ext.at[0, pl.ds(1, 4)], 0, g_up, b)
     send(ext.at[pl.ds(1, 2), 1], ext.at[pl.ds(1, 2), 5], 0, g, b_down)
     send(ext.at[pl.ds(1, 2), 4], ext.at[pl.ds(1, 2), 0], 0, g, b_up)
+
+    tell(0)
 
     loads[1].wait()
     cot_rows = cot_v[...].reshape(128, CH)
@@ -175,6 +186,8 @@
     loads[2].wait()
     loads[3].wait()
 
+    heard(0)
+    tell(1)
     arrived(0)
 
     def clear(outside, part):
@@ -236,7 +249,11 @@
     et_send[...] = matmul_nt(sort, cells).astype(BF16).reshape(4, 32, 384)
     spread_out(lambda mate: et_send.at[mate // 4], et_all, 6)
     et_all[chip, core] = et_send[share]
+    heard(1)
+    tell(2)
     relay(cot_all, 1, 9)
+    heard(2)
+    tell(3)
 
     coarse_halo_wait(cext, 2)
 
@@ -342,6 +359,7 @@
     for brick in range(BRICKS):
         pair = [acc[pl.ds(brick, 8, stride=32), :] for acc in (acc_f, acc_c)]
         rows[brick] = jnp.concatenate(pair, axis=0).astype(BF16)
+    heard(3)
     for high, step, brick in brick_targets(b):
         send(rows.at[brick], sums.at[high * 16 + step], 7, g, brick)
     sums[0] = rows[b]
@@ -417,6 +435,7 @@
             pltpu.SemaphoreType.DMA((4,)),
             pltpu.SemaphoreType.DMA((12,)),
             pltpu.SemaphoreType.DMA((12,)),
+            pltpu.SemaphoreType.REGULAR((4,)),
         ],
         compiler_params=pltpu.CompilerParams(
             collective_id=0, has_side_effects=True, vmem_limit_bytes=60 * 1024 * 1024

time: 52.4 us -> 51.1 us (0.975)
  Pallas kernels: 51.6 us -> 50.3 us
    pallas_call x1, Pallas kernels: 50.9 us -> 49.6 us  [body(): pl.pallas_call(kernel, out_shape=tuple((pltpu.VMEM(shape.shape, shape.dty...]
where the time goes in v4:
time: 51.1 us; the launch traced here: 51 us
  Pallas kernels  50.3 us (98%)
  between operations  0.64 us (1%)
    pallas_call x1, Pallas kernels, body(): pl.pallas_call(kernel, out_shape=tuple((pltpu.VMEM(shape.shape, shape.dty...  49.6 us

profile of v4, /device:TPU:1, one launch (start us, length us, event | category | flops | bytes accessed | tf_op | source)
XLA Modules:
  0.0 51.0 jit_solution(3060085270536678710)
XLA Ops:
  0.6 49.6 %unet_levels.1 = (f32[2,4,16,128]{3,2,1,0:T(8,128)S(1)}, f32[27,4,128]{2,1,0:T(4,128)S(1)}, f32[27,4,128]{2,1,0:T(4,128)S(1)}) custom-call(f32[2,4,16,128]{3,2,1,0:T(8,128)} %field.1, f32[2,4,16,128]{3,2,1,0:T(8,128)} %cot.1, bf16[9,384,128]{2,1,0:T(8,128)(2,1)} %bitcast.2, bf16[9,384,128]{2,1,0:T(8,128)(2,1)} %bitcast.3), custom_call_target="tpu_custom_call" | custom-call | flops 600000000 | bytes 2500000 | tf_op jit(solution)/shard_map/unet_levels/pallas_call | solution.py:406
  50.3 0.7 %copy_out.1 = (f32[2,4,16,128]{3,2,1,0:T(8,128)}, f32[27,4,128]{2,1,0:T(4,128)}, f32[27,4,128]{2,1,0:T(4,128)}) custom-call(f32[2,4,16,128]{3,2,1,0:T(8,128)S(1)} %get-tuple-element.6.output, f32[27,4,128]{2,1,0:T(4,128)S(1)} %get-tuple-element.7.grad_fine, f32[27,4,128]{2,1,0:T(4,128)S(1)} %get-tuple-element.8.grad_coarse), custom_call_target="tpu_custom_call" | custom-call | tf_op jit(solution)/shard_map/copy_out/pallas_call | solution.py:446

commit v5 on v3

--- a/solution.py
+++ b/solution.py
@@ -57,28 +57,22 @@
     return wide.reshape(128, CH)
 
 
-def selection(offset, rows, size_y, size_z):
-    row = iota((rows, 128), 0)
-    cell = iota((rows, 128), 1)
-    step_x, step_y, step_z = offset // 9, (offset // 3) % 3, offset % 3
-    plane = size_y * size_z
-    z = cell % size_z + step_z - 1
-    y = (cell // size_z) % size_y + step_y
-    x = cell // plane + step_x
-    source = (x * (size_y + 2) + y) * size_z + z
-    inside = (z >= 0) & (z < size_z)
-    if size_y == 2:
-        inside = inside & (cell < plane)
-    hit = inside & (row == source) & (offset < 27)
+def selection(offset):
+    row = iota((256, 128), 0)
+    cell = iota((256, 128), 1)
+    step_y, step_z = (offset // 3) % 3, offset % 3
+    z = cell % 16 + step_z - 1
+    source = (cell // 64) * 128 + ((cell // 16) % 4 + step_y) * 16 + z
+    hit = (z >= 0) & (z < 16) & (row == source)
     return jnp.where(hit, 1.0, 0.0).astype(BF16)
 
 
 def kernel(
     field, cot, w_fine, w_coarse, output, grad_fine, grad_coarse,
-    field_v, cot_v, wf_v, wc_v, ext, ext3, pool, wide_pool, cext, gext,
-    et_send, et_all, cot_all, slope_all, ct_send, ct_all, lf, lc, acc_f, acc_c,
+    field_v, cot_v, wf_v, wc_v, ext, ext3, pool, wide_pool, coarse_all, shifted_all, act_all, d_all,
+    et_send, et_all, et_rows, cot_all, slope_all, lf, lc, acc_f, acc_c,
     rows, sums, fin,
-    local_sem, send_sem, recv_sem,
+    local_sem, send_sem, recv_sem, ring_sem,
 ):
     g = lax.axis_index("group")
     b = lax.axis_index("brick")
@@ -99,13 +93,21 @@
     def greet(group, brick):
         pl.semaphore_signal(barrier, inc=1, device_id=(group, brick), device_id_type=pl.DeviceIdType.MESH)
 
-    for brick in brick_targets(b):
-        greet(g, brick[2])
-    for group in (g_up, g_down):
-        for brick in (b_up, b_down):
-            greet(group, brick)
     for m in FAR_FIRST:
-        greet(mates[m], b)
+        for brick in (b_up, b_down, b):
+            greet(mates[m], brick)
+    for step in (4, 3, 2, 1):
+        greet(g, (b + step) % BRICKS)
+        greet(g, (b + BRICKS - step) % BRICKS)
+
+    def tell(stage):
+        for step in (4 * 2**stage, BRICKS - 4 * 2**stage):
+            pl.semaphore_signal(
+                ring_sem.at[stage], inc=1, device_id=(g, (b + step) % BRICKS), device_id_type=pl.DeviceIdType.MESH
+            )
+
+    def heard(stage):
+        pl.semaphore_wait(ring_sem.at[stage], 2)
 
     def copy_to(src, dst, send, recv, group, brick):
         return pltpu.make_async_remote_copy(
@@ -123,10 +125,10 @@
     arrivals = (
         ext.at[pl.ds(0, 4), pl.ds(0, 4)],
         cot_all.at[pl.ds(0, 7), 0],
-        cext.at[pl.ds(0, 10)],
+        wide_pool.at[pl.ds(0, 30 * 8)],
         slope_all.at[pl.ds(0, 7), 0],
-        gext.at[pl.ds(0, 3 * GROUPS - 1)],
-        ct_all.at[pl.ds(0, GROUPS - 1)],
+        coarse_all.at[pl.ds(0, 3 * GROUPS - 1)],
+        d_all.at[pl.ds(0, 8), 0],
         et_all.at[pl.ds(0, 7), 0],
         sums.at[pl.ds(0, BRICKS - 1)],
         fin.at[pl.ds(0, GROUPS - 1)],
@@ -154,7 +156,7 @@
 
     loads[0].wait()
     ext[1:3, 1:5] = field_v[...].astype(BF16)
-    pl.semaphore_wait(barrier, 4 + GROUPS - 1 + BRICKS - 1)
+    pl.semaphore_wait(barrier, 3 * (GROUPS - 1) + 8)
 
     send(ext.at[1, 1], ext.at[3, 5], 0, g_down, b_down)
     send(ext.at[1, 4], ext.at[3, 0], 0, g_down, b_up)
@@ -165,11 +167,21 @@
     send(ext.at[pl.ds(1, 2), 1], ext.at[pl.ds(1, 2), 5], 0, g, b_down)
     send(ext.at[pl.ds(1, 2), 4], ext.at[pl.ds(1, 2), 0], 0, g, b_up)
 
+    tell(0)
+
     loads[1].wait()
     cot_rows = cot_v[...].reshape(128, CH)
     cot_all[chip, core] = cot_rows.astype(BF16)
     spread_out(lambda mate: cot_all.at[chip, core], cot_all, 1)
-    d_coarse = pooled(cot_rows, pool)
+    d_all[chip, core, 1:3] = pooled(cot_rows, pool).reshape(2, 8, CH)
+    for m in FAR_FIRST + (0,):
+        if m % 2 == 0:
+            send(d_all.at[chip, core, 1], d_all.at[chip, core, 3], 2, mates[m], b_down)
+            send(d_all.at[chip, core, 2], d_all.at[chip, core, 0], 2, mates[m], b_up)
+            if m:
+                send(d_all.at[chip, core, pl.ds(1, 2)], d_all.at[chip, core, pl.ds(1, 2)], 2, mates[m], b)
+    for row in (0, 1, 2, 51, 52, 53):
+        coarse_all[row] = jnp.zeros((16, CH), BF16)
     order = iota((CH, CH), 0)
     sort = jnp.where(iota((CH, CH), 1) == 4 * (order % 32) + order // 32, 1.0, 0.0).astype(BF16)
     loads[2].wait()
@@ -186,6 +198,14 @@
     clear(g == GROUPS - 1, slice(3, 4))
     clear(b == 0, (slice(0, 4), slice(0, 1)))
     clear(b == BRICKS - 1, (slice(0, 4), slice(5, 6)))
+
+    cells = ext[1:3].reshape(2, 96, CH)
+    cells = jnp.concatenate([cells, jnp.zeros((2, 32, CH), BF16)], axis=1).reshape(256, CH)
+    cells = matmul_nt(sort, cells).astype(BF16).reshape(4, 32, 256)
+    for x in range(2):
+        et_send[:, x] = cells[:, :, x * 128 : (x + 1) * 128]
+    spread_out(lambda mate: et_send.at[mate // 4], et_all, 6)
+    et_all[chip, core] = et_send[share]
 
     cells = ext[...].reshape(384, CH)
     before, after = neighbours_along_depth(cells.astype(F32), 16)
@@ -201,118 +221,87 @@
     sig = jax.nn.sigmoid(z_fine)
     act_fine = z_fine * sig
     slope_fine = sig * (1.0 + z_fine * (1.0 - sig))
-    coarse = (pooled(act_fine, pool) * 0.125).astype(BF16).astype(F32)
-
-    def coarse_halo(buf, phase):
-        send(buf.at[5], buf.at[11], phase, g_down, b_down)
-        send(buf.at[6], buf.at[8], phase, g_down, b_up)
-        send(buf.at[5], buf.at[3], phase, g_up, b_down)
-        send(buf.at[6], buf.at[0], phase, g_up, b_up)
-        send(buf.at[pl.ds(5, 2)], buf.at[pl.ds(9, 2)], phase, g_down, b)
-        send(buf.at[pl.ds(5, 2)], buf.at[pl.ds(1, 2)], phase, g_up, b)
-        send(buf.at[5], buf.at[7], phase, g, b_down)
-        send(buf.at[6], buf.at[4], phase, g, b_up)
-
-    def coarse_halo_wait(buf, phase):
-        arrived(phase)
-
-        def clear(outside, rows):
-            @pl.when(outside)
-            def _():
-                for row in rows:
-                    buf[row] = jnp.zeros((8, CH), F32)
-
-        clear(g == 0, (0, 1, 2, 3))
-        clear(g == GROUPS - 1, (8, 9, 10, 11))
-        clear(b == 0, (0, 4, 8))
-        clear(b == BRICKS - 1, (3, 7, 11))
-
-    cext[5:7] = coarse.reshape(2, 8, CH)
-    coarse_halo(cext, 2)
+    coarse = (pooled(act_fine, pool) * 0.125).astype(BF16)
+
+    own = (g + 1) * 3
+    coarse_all[own + 1] = coarse
+    for m in FAR_FIRST + (0,):
+        send(coarse_all.at[own + 1], coarse_all.at[own + 2], 4, mates[m], b_down)
+        send(coarse_all.at[own + 1], coarse_all.at[own], 4, mates[m], b_up)
+        if m:
+            send(coarse_all.at[own + 1], coarse_all.at[own + 1], 4, mates[m], b)
 
     slope_all[chip, core] = slope_fine.astype(BF16)
     spread_out(lambda mate: slope_all.at[chip, core], slope_all, 3)
 
-    et_send[...] = matmul_nt(sort, cells).astype(BF16).reshape(4, 32, 384)
-    spread_out(lambda mate: et_send.at[mate // 4], et_all, 6)
-    et_all[chip, core] = et_send[share]
+    heard(0)
+    tell(1)
     relay(cot_all, 1, 9)
-
-    coarse_halo_wait(cext, 2)
-
-    ccells = cext[...].reshape(96, CH)
-    before, after = neighbours_along_depth(ccells, 8)
-    wide = jnp.concatenate([before, ccells, after], axis=1)
-    z_coarse = jnp.zeros((16, CH), F32)
-    for step in range(9):
-        start = (step // 3) * 32 + (step % 3) * 8
-        window = wide[start : start + 16].astype(BF16)
-        z_coarse = z_coarse + jnp.dot(window, wc_v[step], preferred_element_type=F32)
-    sig = jax.nn.sigmoid(z_coarse)
-    act_coarse = z_coarse * sig
-    g_coarse = d_coarse * (sig * (1.0 + z_coarse * (1.0 - sig)))
-    g_coarse = g_coarse.astype(BF16)
-
-    own = (g + 1) * 3
-    gext[own + 1] = g_coarse
-    for m in FAR_FIRST + (0,):
-        send(gext.at[own + 1], gext.at[own + 2], 4, mates[m], b_down)
-        send(gext.at[own + 1], gext.at[own], 4, mates[m], b_up)
-        if m:
-            send(gext.at[own + 1], gext.at[own + 1], 4, mates[m], b)
-    for row in (0, 1, 2, 51, 52, 53):
-        gext[row] = jnp.zeros((16, CH), BF16)
-
-    ccells = jnp.concatenate([ccells, jnp.zeros((32, CH), F32)], axis=0).astype(BF16)
-    ct_send[...] = matmul_nt(sort, ccells).astype(BF16).reshape(4, 32, 128)
-    for m in FAR_FIRST:
-        send(ct_send.at[mates[m] // 4], ct_all.at[g], 5, mates[m], b)
-    ct_all[g] = ct_send[share]
-
-    output[...] = (act_fine + spread(act_coarse, pool)).reshape(2, 4, 16, CH)
-
+    relay(d_all, 2, 5)
+    relay(et_all, 6, 11)
     relay(slope_all, 3, 10)
-    relay(et_all, 6, 11)
+
+    def offset_of(step):
+        return quarter * PART + step - (quarter // 3 if step == PART - 1 else 0)
 
     arrived(11)
-    everyone = et_all[...].reshape(GROUPS * 32, 384)
-    for k in range(0, PART, 2):
-        steps = range(k, min(k + 2, PART))
-        chosen = [selection(quarter * PART + step, 384, 4, 16) for step in steps]
-        picked = jnp.dot(everyone, jnp.concatenate(chosen, axis=1), preferred_element_type=F32)
-        picked = picked.astype(BF16).reshape(8, 2, 32, len(chosen) * 128)
-        for i, step in enumerate(steps):
-            for half in range(2):
-                lf[:, step, :, half * 128 : (half + 1) * 128] = picked[:, half, :, i * 128 : (i + 1) * 128]
+    et_rows[0] = jnp.zeros((32, 128), BF16)
+    et_rows[2 * GROUPS + 1] = jnp.zeros((32, 128), BF16)
+    et_rows[1 : 2 * GROUPS + 1] = et_all[...].reshape(2 * GROUPS, 32, 128)
+    for step in range(PART):
+        offset = offset_of(step)
+        pairs = et_rows[pl.ds(offset // 9, 2 * GROUPS)].reshape(GROUPS, 2, 32, 128)
+        pairs = jnp.concatenate([pairs[:, 0], pairs[:, 1]], axis=2).reshape(GROUPS * 32, 256)
+        picked = jnp.dot(pairs, selection(offset), preferred_element_type=F32)
+        picked = picked.astype(BF16).reshape(8, 2, 32, 128)
+        for half in range(2):
+            lf[:, step, :, half * 128 : (half + 1) * 128] = picked[:, half]
+    arrived(9)
     arrived(5)
-    everyone = ct_all[...].reshape(GROUPS * 32, 128)
-    for k in range(0, PART, 2):
-        steps = range(k, min(k + 2, PART))
-        chosen = [selection(quarter * PART + step, 128, 2, 8) for step in steps]
-        picked = jnp.dot(everyone, jnp.concatenate(chosen, axis=1), preferred_element_type=F32)
-        picked = picked.astype(BF16).reshape(8, 2, 32, len(chosen) * 128)
-        for i, step in enumerate(steps):
-            for half in range(2):
-                lc[:, step, :, half * 128 : (half + 1) * 128] = picked[:, half, :, i * 128 : (i + 1) * 128]
-    arrived(9)
     arrived(10)
-
     arrived(4)
 
-    def clear_gext(outside, place):
+    def clear_sides(outside, place):
         @pl.when(outside)
         def _():
             for x in range(GROUPS):
-                gext[(x + 1) * 3 + place] = jnp.zeros((16, CH), BF16)
-
-    clear_gext(b == 0, 0)
-    clear_gext(b == BRICKS - 1, 2)
-
-    gcells = gext[...].astype(F32).reshape(GROUPS + 2, 6, 8, CH)
+                coarse_all[(x + 1) * 3 + place] = jnp.zeros((16, CH), BF16)
+
+    clear_sides(b == 0, 0)
+    clear_sides(b == BRICKS - 1, 2)
+
+    ccells = coarse_all[...].astype(F32).reshape((GROUPS + 2) * 48, CH)
+    before, after = neighbours_along_depth(ccells, 8)
+    for step_z, shifted in enumerate((before, ccells, after)):
+        shifted = shifted.reshape(GROUPS + 2, 6, 8, CH)
+        for y in range(5):
+            shifted_all[step_z, :, y] = shifted[:, y : y + 2].reshape(GROUPS + 2, 16, CH).astype(BF16)
+    z_coarse = jnp.zeros((GROUPS * 32, CH), F32)
+    for step in range(9):
+        step_x, step_y = step // 3, step % 3
+        window = [
+            jnp.concatenate(
+                [shifted_all[step_z, step_x : step_x + GROUPS, step_y + y][:, None] for y in (0, 2)], axis=1
+            ).reshape(GROUPS * 32, CH)
+            for step_z in range(3)
+        ]
+        window = jnp.concatenate(window, axis=1)
+        z_coarse = z_coarse + jnp.dot(window, wc_v[step], preferred_element_type=F32)
+    sig = jax.nn.sigmoid(z_coarse)
+    act_all[...] = (z_coarse * sig).reshape(GROUPS, 32, CH)
+    d_coarse = d_all[...].reshape(GROUPS * 32, CH)
+    row = iota((GROUPS * 32, CH), 0) % 32
+    outside = ((row < 8) & (b == 0)) | ((row >= 24) & (b == BRICKS - 1))
+    d_coarse = jnp.where(outside, 0.0, d_coarse)
+    g_coarse = d_coarse * (sig * (1.0 + z_coarse * (1.0 - sig)))
+    g_coarse = g_coarse.astype(BF16).astype(F32).reshape(GROUPS, 4, 8, CH)
+
+    empty = jnp.zeros((1, 4, 8, CH), F32)
+    gcells = jnp.concatenate([empty, g_coarse, empty], axis=0)
     mixed = jnp.zeros((GROUPS * 16, 3 * CH), F32)
     for step in range(9):
         step_x, step_y = step // 3, step % 3
-        window = gcells[2 - step_x : 18 - step_x, 3 - step_y : 5 - step_y].reshape(GROUPS * 16, CH)
+        window = gcells[2 - step_x : 18 - step_x, 2 - step_y : 4 - step_y].reshape(GROUPS * 16, CH)
         mixed = mixed + matmul_nt(window.astype(BF16), wc_v[step])
     back_coarse = mixed[:, CH : 2 * CH]
     back_coarse = back_coarse + neighbours_along_depth(mixed[:, 0:CH], 8)[1]
@@ -329,22 +318,26 @@
         total = total + jnp.dot(lf[pair].reshape(PART * 32, 256), grads, preferred_element_type=F32)
     acc_f[0 : PART * 32] = total
 
-    total = jnp.zeros((PART * 32, CH), F32)
-    empty = jnp.zeros((112, CH), BF16)
-    for pair in range(8):
-        first, second = (gext[(2 * pair + i + 1) * 3 + 1] for i in range(2))
-        grads = jnp.concatenate([first, empty, second, empty], axis=0)
-        total = total + jnp.dot(lc[pair].reshape(PART * 32, 256), grads, preferred_element_type=F32)
-    acc_c[0 : PART * 32] = total
+    row = iota((32, CH), 0)
+    own_class = jnp.where(iota((32, CH), 1) == 4 * row + share, 1.0, 0.0).astype(BF16)
+    for step in range(PART):
+        offset = offset_of(step)
+        step_x, step_y, step_z = offset // 9, (offset // 3) % 3, offset % 3
+        window = shifted_all[step_z, pl.ds(step_x, GROUPS), step_y + 1].reshape(GROUPS * 16, CH)
+        lc[step] = matmul_nt(own_class, window).astype(BF16)
+    grads = g_coarse[:, 1:3].reshape(GROUPS * 16, CH).astype(BF16)
+    acc_c[0 : PART * 32] = jnp.dot(lc[...].reshape(PART * 32, 256), grads, preferred_element_type=F32)
     acc_c[PART * 32 :] = jnp.zeros((32, CH), F32)
     acc_f[PART * 32 :] = jnp.zeros((32, CH), F32)
 
     for brick in range(BRICKS):
         pair = [acc[pl.ds(brick, 8, stride=32), :] for acc in (acc_f, acc_c)]
         rows[brick] = jnp.concatenate(pair, axis=0).astype(BF16)
+    heard(1)
     for high, step, brick in brick_targets(b):
         send(rows.at[brick], sums.at[high * 16 + step], 7, g, brick)
     sums[0] = rows[b]
+    output[...] = (act_fine + spread(act_all[g, 8:24], pool)).reshape(2, 4, 16, CH)
     arrived(7)
     fin[g] = jnp.sum(sums[...].astype(F32), axis=0)
     for m in FAR_FIRST:
@@ -399,16 +392,17 @@
             pltpu.VMEM((4, 6, 16, 3 * CH), BF16),
             pltpu.VMEM((32, CH), F32),
             pltpu.VMEM((GROUPS * 32, CH), F32),
-            pltpu.VMEM((12, 8, CH), F32),
             pltpu.VMEM(((GROUPS + 2) * 3, 16, CH), BF16),
-            pltpu.VMEM((4, 32, 384), BF16),
-            pltpu.VMEM((8, 2, 32, 384), BF16),
+            pltpu.VMEM((3, GROUPS + 2, 5, 16, CH), BF16),
+            pltpu.VMEM((GROUPS, 32, CH), F32),
+            pltpu.VMEM((8, 2, 4, 8, CH), F32),
+            pltpu.VMEM((4, 2, 32, 128), BF16),
+            pltpu.VMEM((8, 2, 2, 32, 128), BF16),
+            pltpu.VMEM((2 * GROUPS + 2, 32, 128), BF16),
             pltpu.VMEM((8, 2, 128, CH), BF16),
             pltpu.VMEM((8, 2, 128, CH), BF16),
-            pltpu.VMEM((4, 32, 128), BF16),
-            pltpu.VMEM((GROUPS, 32, 128), BF16),
             pltpu.VMEM((8, PART, 32, 256), BF16),
-            pltpu.VMEM((8, PART, 32, 256), BF16),
+            pltpu.VMEM((PART, 32, 256), BF16),
             pltpu.VMEM((256, CH), F32),
             pltpu.VMEM((256, CH), F32),
             pltpu.VMEM((BRICKS, 16, CH), BF16),
@@ -417,6 +411,7 @@
             pltpu.SemaphoreType.DMA((4,)),
             pltpu.SemaphoreType.DMA((12,)),
             pltpu.SemaphoreType.DMA((12,)),
+            pltpu.SemaphoreType.REGULAR((2,)),
         ],
         compiler_params=pltpu.CompilerParams(
             collective_id=0, has_side_effects=True, vmem_limit_bytes=60 * 1024 * 1024

time: 52.4 us -> 50.1 us (0.956)
  Pallas kernels: 51.6 us -> 49.4 us
    pallas_call x1, Pallas kernels: 50.9 us -> 48.7 us  [body(): pl.pallas_call(kernel, out_shape=tuple((pltpu.VMEM(shape.shape, shape.dty...]
where the time goes in v5:
time: 50.1 us; the launch traced here: 50 us
  Pallas kernels  49.4 us (99%)
  between operations  0.64 us (1%)
    pallas_call x1, Pallas kernels, body(): pl.pallas_call(kernel, out_shape=tuple((pltpu.VMEM(shape.shape, shape.dty...  48.7 us

profile of v5, /device:TPU:1, one launch (start us, length us, event | category | flops | bytes accessed | tf_op | source)
XLA Modules:
  0.0 50.0 jit_solution(5007804363713299047)
XLA Ops:
  0.6 48.7 %unet_levels.1 = (f32[2,4,16,128]{3,2,1,0:T(8,128)S(1)}, f32[27,4,128]{2,1,0:T(4,128)S(1)}, f32[27,4,128]{2,1,0:T(4,128)S(1)}) custom-call(f32[2,4,16,128]{3,2,1,0:T(8,128)} %field.1, f32[2,4,16,128]{3,2,1,0:T(8,128)} %cot.1, bf16[9,384,128]{2,1,0:T(8,128)(2,1)} %bitcast.2, bf16[9,384,128]{2,1,0:T(8,128)(2,1)} %bitcast.3), custom_call_target="tpu_custom_call" | custom-call | flops 600000000 | bytes 2500000 | tf_op jit(solution)/shard_map/unet_levels/pallas_call | solution.py:381
  49.3 0.7 %copy_out.1 = (f32[2,4,16,128]{3,2,1,0:T(8,128)}, f32[27,4,128]{2,1,0:T(4,128)}, f32[27,4,128]{2,1,0:T(4,128)}) custom-call(f32[2,4,16,128]{3,2,1,0:T(8,128)S(1)} %get-tuple-element.6.output, f32[27,4,128]{2,1,0:T(4,128)S(1)} %get-tuple-element.7.grad_fine, f32[27,4,128]{2,1,0:T(4,128)S(1)} %get-tuple-element.8.grad_coarse), custom_call_target="tpu_custom_call" | custom-call | tf_op jit(solution)/shard_map/copy_out/pallas_call | solution.py:422

commit v6 on v5

--- a/solution.py
+++ b/solution.py
@@ -58,19 +58,19 @@
 
 
 def selection(offset):
-    row = iota((256, 128), 0)
-    cell = iota((256, 128), 1)
-    step_y, step_z = (offset // 3) % 3, offset % 3
+    row = iota((384, 128), 0)
+    cell = iota((384, 128), 1)
+    step_x, step_y, step_z = offset // 9, (offset // 3) % 3, offset % 3
     z = cell % 16 + step_z - 1
-    source = (cell // 64) * 128 + ((cell // 16) % 4 + step_y) * 16 + z
+    source = (cell // 64 + step_x) * 96 + ((cell // 16) % 4 + step_y) * 16 + z
     hit = (z >= 0) & (z < 16) & (row == source)
     return jnp.where(hit, 1.0, 0.0).astype(BF16)
 
 
 def kernel(
     field, cot, w_fine, w_coarse, output, grad_fine, grad_coarse,
-    field_v, cot_v, wf_v, wc_v, ext, ext3, pool, wide_pool, coarse_all, shifted_all, act_all, d_all,
-    et_send, et_all, et_rows, cot_all, slope_all, lf, lc, acc_f, acc_c,
+    field_v, cot_v, wf_v, wc_v, ext, ext3, pool, wide_pool, coarse_all, shifted_all, act_all, d_all, g_pairs,
+    et_send, et_all, chosen, cot_all, slope_all, lf, lc, both, swapped, acc_f, acc_c,
     rows, sums, fin,
     local_sem, send_sem, recv_sem, ring_sem,
 ):
@@ -124,17 +124,15 @@
 
     arrivals = (
         ext.at[pl.ds(0, 4), pl.ds(0, 4)],
-        cot_all.at[pl.ds(0, 7), 0],
+        cot_all.at[pl.ds(0, 7)],
         wide_pool.at[pl.ds(0, 30 * 8)],
-        slope_all.at[pl.ds(0, 7), 0],
+        slope_all.at[pl.ds(0, 7)],
         coarse_all.at[pl.ds(0, 3 * GROUPS - 1)],
         d_all.at[pl.ds(0, 8), 0],
-        et_all.at[pl.ds(0, 7), 0],
+        et_all.at[pl.ds(0, 7)],
         sums.at[pl.ds(0, BRICKS - 1)],
         fin.at[pl.ds(0, GROUPS - 1)],
-        cot_all.at[pl.ds(0, 8), 0],
-        slope_all.at[pl.ds(0, 8), 0],
-        et_all.at[pl.ds(0, 8), 0],
+        swapped.at[pl.ds(0, PART * 32)],
     )
 
     def arrived(phase):
@@ -148,11 +146,7 @@
     def spread_out(src_of, buf, phase):
         for m in FAR_FIRST:
             if m % 2 == 0:
-                send(src_of(mates[m]), buf.at[chip, core], phase, mates[m], b)
-
-    def relay(buf, phase, after):
-        arrived(phase)
-        send(buf.at[:, core], buf.at[:, core], after, mates[1], b)
+                send(src_of(mates[m]), buf.at[chip], phase, mates[m], b)
 
     loads[0].wait()
     ext[1:3, 1:5] = field_v[...].astype(BF16)
@@ -171,8 +165,8 @@
 
     loads[1].wait()
     cot_rows = cot_v[...].reshape(128, CH)
-    cot_all[chip, core] = cot_rows.astype(BF16)
-    spread_out(lambda mate: cot_all.at[chip, core], cot_all, 1)
+    cot_all[chip] = cot_rows.astype(BF16)
+    spread_out(lambda mate: cot_all.at[chip], cot_all, 1)
     d_all[chip, core, 1:3] = pooled(cot_rows, pool).reshape(2, 8, CH)
     for m in FAR_FIRST + (0,):
         if m % 2 == 0:
@@ -184,6 +178,15 @@
         coarse_all[row] = jnp.zeros((16, CH), BF16)
     order = iota((CH, CH), 0)
     sort = jnp.where(iota((CH, CH), 1) == 4 * (order % 32) + order // 32, 1.0, 0.0).astype(BF16)
+    def offset_of(step):
+        return quarter * PART + step - (quarter // 3 if step == PART - 1 else 0)
+
+    half = quarter // 2
+    for step in range(0, 2 * PART, 2):
+        offset = half * 2 * PART + step
+        later = offset + 1 - (half if step + 1 == 2 * PART - 1 else 0)
+        chosen[step // 2, :, 0:128] = selection(offset)
+        chosen[step // 2, :, 128:256] = selection(later)
     loads[2].wait()
     loads[3].wait()
 
@@ -199,15 +202,11 @@
     clear(b == 0, (slice(0, 4), slice(0, 1)))
     clear(b == BRICKS - 1, (slice(0, 4), slice(5, 6)))
 
-    cells = ext[1:3].reshape(2, 96, CH)
-    cells = jnp.concatenate([cells, jnp.zeros((2, 32, CH), BF16)], axis=1).reshape(256, CH)
-    cells = matmul_nt(sort, cells).astype(BF16).reshape(4, 32, 256)
-    for x in range(2):
-        et_send[:, x] = cells[:, :, x * 128 : (x + 1) * 128]
+    cells = ext[...].reshape(384, CH)
+    et_send[...] = matmul_nt(sort, cells).astype(BF16).reshape(4, 32, 384)
     spread_out(lambda mate: et_send.at[mate // 4], et_all, 6)
-    et_all[chip, core] = et_send[share]
-
-    cells = ext[...].reshape(384, CH)
+    et_all[chip] = et_send[share]
+
     before, after = neighbours_along_depth(cells.astype(F32), 16)
     ext3[:, :, :, 0:CH] = before.astype(BF16).reshape(4, 6, 16, CH)
     ext3[:, :, :, CH : 2 * CH] = ext[...]
@@ -231,34 +230,23 @@
         if m:
             send(coarse_all.at[own + 1], coarse_all.at[own + 1], 4, mates[m], b)
 
-    slope_all[chip, core] = slope_fine.astype(BF16)
-    spread_out(lambda mate: slope_all.at[chip, core], slope_all, 3)
+    slope_all[chip] = slope_fine.astype(BF16)
+    spread_out(lambda mate: slope_all.at[chip], slope_all, 3)
 
     heard(0)
     tell(1)
-    relay(cot_all, 1, 9)
-    relay(d_all, 2, 5)
-    relay(et_all, 6, 11)
-    relay(slope_all, 3, 10)
-
-    def offset_of(step):
-        return quarter * PART + step - (quarter // 3 if step == PART - 1 else 0)
-
-    arrived(11)
-    et_rows[0] = jnp.zeros((32, 128), BF16)
-    et_rows[2 * GROUPS + 1] = jnp.zeros((32, 128), BF16)
-    et_rows[1 : 2 * GROUPS + 1] = et_all[...].reshape(2 * GROUPS, 32, 128)
-    for step in range(PART):
-        offset = offset_of(step)
-        pairs = et_rows[pl.ds(offset // 9, 2 * GROUPS)].reshape(GROUPS, 2, 32, 128)
-        pairs = jnp.concatenate([pairs[:, 0], pairs[:, 1]], axis=2).reshape(GROUPS * 32, 256)
-        picked = jnp.dot(pairs, selection(offset), preferred_element_type=F32)
-        picked = picked.astype(BF16).reshape(8, 2, 32, 128)
-        for half in range(2):
-            lf[:, step, :, half * 128 : (half + 1) * 128] = picked[:, half]
-    arrived(9)
+    arrived(2)
+    send(d_all.at[:, core], d_all.at[:, core], 5, mates[1], b)
+
+    arrived(6)
+    everyone = et_all[...].reshape(8 * 32, 384)
+    for step in range(0, 2 * PART, 2):
+        picked = jnp.dot(everyone, chosen[step // 2], preferred_element_type=F32).astype(BF16).reshape(4, 2, 32, 256)
+        for i in range(2):
+            for member in range(2):
+                lf[:, step + i, :, member * 128 : (member + 1) * 128] = picked[:, member, :, i * 128 : (i + 1) * 128]
+    arrived(1)
     arrived(5)
-    arrived(10)
     arrived(4)
 
     def clear_sides(outside, place):
@@ -295,28 +283,35 @@
     d_coarse = jnp.where(outside, 0.0, d_coarse)
     g_coarse = d_coarse * (sig * (1.0 + z_coarse * (1.0 - sig)))
     g_coarse = g_coarse.astype(BF16).astype(F32).reshape(GROUPS, 4, 8, CH)
-
-    empty = jnp.zeros((1, 4, 8, CH), F32)
-    gcells = jnp.concatenate([empty, g_coarse, empty], axis=0)
-    mixed = jnp.zeros((GROUPS * 16, 3 * CH), F32)
+    g_pairs[0] = jnp.zeros((3, 16, CH), BF16)
+    g_pairs[GROUPS + 1] = jnp.zeros((3, 16, CH), BF16)
+    for y in range(3):
+        g_pairs[1 : GROUPS + 1, y] = g_coarse[:, y : y + 2].reshape(GROUPS, 16, CH).astype(BF16)
+
+    mixed = jnp.zeros((8 * 16, 3 * CH), F32)
     for step in range(9):
         step_x, step_y = step // 3, step % 3
-        window = gcells[2 - step_x : 18 - step_x, 2 - step_y : 4 - step_y].reshape(GROUPS * 16, CH)
-        mixed = mixed + matmul_nt(window.astype(BF16), wc_v[step])
+        window = jnp.concatenate([g_pairs[2 * member + core + 2 - step_x, 2 - step_y] for member in range(8)], axis=0)
+        mixed = mixed + matmul_nt(window, wc_v[step])
     back_coarse = mixed[:, CH : 2 * CH]
     back_coarse = back_coarse + neighbours_along_depth(mixed[:, 0:CH], 8)[1]
     back_coarse = back_coarse + neighbours_along_depth(mixed[:, 2 * CH :], 8)[0]
     back_coarse = back_coarse * 0.125
-    wide_pool[pl.ds(0, GROUPS * 16, stride=2), :] = back_coarse
-    wide_pool[pl.ds(1, GROUPS * 16, stride=2), :] = back_coarse
-    total = jnp.zeros((PART * 32, CH), F32)
-    for pair in range(8):
-        back = wide_pool[pair * 64 : (pair + 1) * 64].reshape(2, 1, 2, 1, 16, CH)
-        back = jnp.broadcast_to(back, (2, 2, 2, 2, 16, CH)).reshape(256, CH)
-        grads = cot_all[pair].reshape(256, CH).astype(F32) + back
-        grads = (grads * slope_all[pair].reshape(256, CH).astype(F32)).astype(BF16)
-        total = total + jnp.dot(lf[pair].reshape(PART * 32, 256), grads, preferred_element_type=F32)
-    acc_f[0 : PART * 32] = total
+    wide_pool[pl.ds(0, 8 * 16, stride=2), :] = back_coarse
+    wide_pool[pl.ds(1, 8 * 16, stride=2), :] = back_coarse
+    arrived(3)
+    total = jnp.zeros((2 * PART * 32, CH), F32)
+    for pair in range(4):
+        grads = []
+        for member in (2 * pair, 2 * pair + 1):
+            back = wide_pool[member * 32 : (member + 1) * 32].reshape(1, 2, 1, 16, CH)
+            back = jnp.broadcast_to(back, (2, 2, 2, 16, CH)).reshape(128, CH)
+            fine = cot_all[member].astype(F32) + back
+            grads.append((fine * slope_all[member].astype(F32)).astype(BF16))
+        grads = jnp.concatenate(grads, axis=0)
+        total = total + jnp.dot(lf[pair].reshape(2 * PART * 32, 256), grads, preferred_element_type=F32)
+    both[...] = total.reshape(2, PART * 32, CH)
+    send(both.at[1 - core], swapped, 9, mates[1], b)
 
     row = iota((32, CH), 0)
     own_class = jnp.where(iota((32, CH), 1) == 4 * row + share, 1.0, 0.0).astype(BF16)
@@ -325,8 +320,10 @@
         step_x, step_y, step_z = offset // 9, (offset // 3) % 3, offset % 3
         window = shifted_all[step_z, pl.ds(step_x, GROUPS), step_y + 1].reshape(GROUPS * 16, CH)
         lc[step] = matmul_nt(own_class, window).astype(BF16)
-    grads = g_coarse[:, 1:3].reshape(GROUPS * 16, CH).astype(BF16)
+    grads = g_pairs[1 : GROUPS + 1, 1].reshape(GROUPS * 16, CH)
     acc_c[0 : PART * 32] = jnp.dot(lc[...].reshape(PART * 32, 256), grads, preferred_element_type=F32)
+    arrived(9)
+    acc_f[0 : PART * 32] = both[core] + swapped[...]
     acc_c[PART * 32 :] = jnp.zeros((32, CH), F32)
     acc_f[PART * 32 :] = jnp.zeros((32, CH), F32)
 
@@ -343,7 +340,7 @@
     for m in FAR_FIRST:
         send(fin.at[g], fin.at[g], 8, mates[m], b)
 
-    for phase in (0, 1, 2, 3, 4, 5, 6, 7, 9, 10, 11):
+    for phase in (0, 1, 2, 3, 4, 5, 6, 7, 9):
         sent(phase)
 
     arrived(8)
@@ -391,26 +388,29 @@
             pltpu.VMEM((4, 6, 16, CH), BF16),
             pltpu.VMEM((4, 6, 16, 3 * CH), BF16),
             pltpu.VMEM((32, CH), F32),
-            pltpu.VMEM((GROUPS * 32, CH), F32),
+            pltpu.VMEM((8 * 32, CH), F32),
             pltpu.VMEM(((GROUPS + 2) * 3, 16, CH), BF16),
             pltpu.VMEM((3, GROUPS + 2, 5, 16, CH), BF16),
             pltpu.VMEM((GROUPS, 32, CH), F32),
             pltpu.VMEM((8, 2, 4, 8, CH), F32),
-            pltpu.VMEM((4, 2, 32, 128), BF16),
-            pltpu.VMEM((8, 2, 2, 32, 128), BF16),
-            pltpu.VMEM((2 * GROUPS + 2, 32, 128), BF16),
-            pltpu.VMEM((8, 2, 128, CH), BF16),
-            pltpu.VMEM((8, 2, 128, CH), BF16),
-            pltpu.VMEM((8, PART, 32, 256), BF16),
+            pltpu.VMEM((GROUPS + 2, 3, 16, CH), BF16),
+            pltpu.VMEM((4, 32, 384), BF16),
+            pltpu.VMEM((8, 32, 384), BF16),
+            pltpu.VMEM((PART, 384, 256), BF16),
+            pltpu.VMEM((8, 128, CH), BF16),
+            pltpu.VMEM((8, 128, CH), BF16),
+            pltpu.VMEM((4, 2 * PART, 32, 256), BF16),
             pltpu.VMEM((PART, 32, 256), BF16),
+            pltpu.VMEM((2, PART * 32, CH), F32),
+            pltpu.VMEM((PART * 32, CH), F32),
             pltpu.VMEM((256, CH), F32),
             pltpu.VMEM((256, CH), F32),
             pltpu.VMEM((BRICKS, 16, CH), BF16),
             pltpu.VMEM((BRICKS, 16, CH), BF16),
             pltpu.VMEM((GROUPS, 16, CH), F32),
             pltpu.SemaphoreType.DMA((4,)),
-            pltpu.SemaphoreType.DMA((12,)),
-            pltpu.SemaphoreType.DMA((12,)),
+            pltpu.SemaphoreType.DMA((10,)),
+            pltpu.SemaphoreType.DMA((10,)),
             pltpu.SemaphoreType.REGULAR((2,)),
         ],
         compiler_params=pltpu.CompilerParams(

time: 50.1 us -> 49.3 us (0.984)
  Pallas kernels: 49.4 us -> 48.5 us
    pallas_call x1, Pallas kernels: 48.7 us -> 47.9 us  [body(): pl.pallas_call(kernel, out_shape=tuple((pltpu.VMEM(shape.shape, shape.dty...]
where the time goes in v6:
time: 49.3 us; the launch traced here: 49.2 us
  Pallas kernels  48.5 us (98%)
  between operations  0.64 us (1%)
    pallas_call x1, Pallas kernels, body(): pl.pallas_call(kernel, out_shape=tuple((pltpu.VMEM(shape.shape, shape.dty...  47.9 us

profile of v6, /device:TPU:1, one launch (start us, length us, event | category | flops | bytes accessed | tf_op | source)
XLA Modules:
  0.0 49.2 jit_solution(15403984349181309600)
XLA Ops:
  0.6 47.9 %unet_levels.1 = (f32[2,4,16,128]{3,2,1,0:T(8,128)S(1)}, f32[27,4,128]{2,1,0:T(4,128)S(1)}, f32[27,4,128]{2,1,0:T(4,128)S(1)}) custom-call(f32[2,4,16,128]{3,2,1,0:T(8,128)} %field.1, f32[2,4,16,128]{3,2,1,0:T(8,128)} %cot.1, bf16[9,384,128]{2,1,0:T(8,128)(2,1)} %bitcast.2, bf16[9,384,128]{2,1,0:T(8,128)(2,1)} %bitcast.3), custom_call_target="tpu_custom_call" | custom-call | flops 600000000 | bytes 2500000 | tf_op jit(solution)/shard_map/unet_levels/pallas_call | solution.py:378
  48.5 0.7 %copy_out.1 = (f32[2,4,16,128]{3,2,1,0:T(8,128)}, f32[27,4,128]{2,1,0:T(4,128)}, f32[27,4,128]{2,1,0:T(4,128)}) custom-call(f32[2,4,16,128]{3,2,1,0:T(8,128)S(1)} %get-tuple-element.6.output, f32[27,4,128]{2,1,0:T(4,128)S(1)} %get-tuple-element.7.grad_fine, f32[27,4,128]{2,1,0:T(4,128)S(1)} %get-tuple-element.8.grad_coarse), custom_call_target="tpu_custom_call" | custom-call | tf_op jit(solution)/shard_map/copy_out/pallas_call | solution.py:422

commit v7 on v6

--- a/solution.py
+++ b/solution.py
@@ -60,17 +60,21 @@
 def selection(offset):
     row = iota((384, 128), 0)
     cell = iota((384, 128), 1)
-    step_x, step_y, step_z = offset // 9, (offset // 3) % 3, offset % 3
-    z = cell % 16 + step_z - 1
-    source = (cell // 64 + step_x) * 96 + ((cell // 16) % 4 + step_y) * 16 + z
-    hit = (z >= 0) & (z < 16) & (row == source)
+    z = cell % 16 + offset % 3 - 1
+    y = (cell // 16) % 4 + (offset // 3) % 3
+    x = cell // 64 + offset // 9
+    own = ((x - 1) * 4 + y - 1) * 16
+    side = 320 + (x - 1) * 32 + jnp.where(y == 5, 16, 0)
+    source = jnp.where((y == 0) | (y == 5), side, own)
+    source = jnp.where(x == 0, 128 + y * 16, jnp.where(x == 3, 224 + y * 16, source))
+    hit = (z >= 0) & (z < 16) & (row == source + z)
     return jnp.where(hit, 1.0, 0.0).astype(BF16)
 
 
 def kernel(
     field, cot, w_fine, w_coarse, output, grad_fine, grad_coarse,
     field_v, cot_v, wf_v, wc_v, ext, ext3, pool, wide_pool, coarse_all, shifted_all, act_all, d_all, g_pairs,
-    et_send, et_all, chosen, cot_all, slope_all, lf, lc, both, swapped, acc_f, acc_c,
+    own_send, own_all, rim_send, rim_all, chosen, cot_all, slope_all, lf, lc, both, swapped, acc_f, acc_c,
     rows, sums, fin,
     local_sem, send_sem, recv_sem, ring_sem,
 ):
@@ -129,10 +133,11 @@
         slope_all.at[pl.ds(0, 7)],
         coarse_all.at[pl.ds(0, 3 * GROUPS - 1)],
         d_all.at[pl.ds(0, 8), 0],
-        et_all.at[pl.ds(0, 7)],
+        rim_all.at[pl.ds(0, 7)],
         sums.at[pl.ds(0, BRICKS - 1)],
         fin.at[pl.ds(0, GROUPS - 1)],
         swapped.at[pl.ds(0, PART * 32)],
+        own_all.at[pl.ds(0, 7)],
     )
 
     def arrived(phase):
@@ -178,6 +183,10 @@
         coarse_all[row] = jnp.zeros((16, CH), BF16)
     order = iota((CH, CH), 0)
     sort = jnp.where(iota((CH, CH), 1) == 4 * (order % 32) + order // 32, 1.0, 0.0).astype(BF16)
+    own_send[...] = matmul_nt(sort, ext[1:3, 1:5].reshape(128, CH)).astype(BF16).reshape(4, 32, 128)
+    spread_out(lambda mate: own_send.at[mate // 4], own_all, 10)
+    own_all[chip] = own_send[share]
+
     def offset_of(step):
         return quarter * PART + step - (quarter // 3 if step == PART - 1 else 0)
 
@@ -203,9 +212,10 @@
     clear(b == BRICKS - 1, (slice(0, 4), slice(5, 6)))
 
     cells = ext[...].reshape(384, CH)
-    et_send[...] = matmul_nt(sort, cells).astype(BF16).reshape(4, 32, 384)
-    spread_out(lambda mate: et_send.at[mate // 4], et_all, 6)
-    et_all[chip] = et_send[share]
+    rim = [ext[0].reshape(96, CH), ext[3].reshape(96, CH), ext[1, 0], ext[1, 5], ext[2, 0], ext[2, 5]]
+    rim_send[...] = matmul_nt(sort, jnp.concatenate(rim, axis=0)).astype(BF16).reshape(4, 32, 256)
+    spread_out(lambda mate: rim_send.at[mate // 4], rim_all, 6)
+    rim_all[chip] = rim_send[share]
 
     before, after = neighbours_along_depth(cells.astype(F32), 16)
     ext3[:, :, :, 0:CH] = before.astype(BF16).reshape(4, 6, 16, CH)
@@ -238,8 +248,9 @@
     arrived(2)
     send(d_all.at[:, core], d_all.at[:, core], 5, mates[1], b)
 
+    arrived(10)
     arrived(6)
-    everyone = et_all[...].reshape(8 * 32, 384)
+    everyone = jnp.concatenate([own_all[...], rim_all[...]], axis=2).reshape(8 * 32, 384)
     for step in range(0, 2 * PART, 2):
         picked = jnp.dot(everyone, chosen[step // 2], preferred_element_type=F32).astype(BF16).reshape(4, 2, 32, 256)
         for i in range(2):
@@ -327,12 +338,16 @@
     acc_c[PART * 32 :] = jnp.zeros((32, CH), F32)
     acc_f[PART * 32 :] = jnp.zeros((32, CH), F32)
 
-    for brick in range(BRICKS):
+    heard(1)
+
+    def chunk(brick):
         pair = [acc[pl.ds(brick, 8, stride=32), :] for acc in (acc_f, acc_c)]
         rows[brick] = jnp.concatenate(pair, axis=0).astype(BF16)
-    heard(1)
+
     for high, step, brick in brick_targets(b):
+        chunk(brick)
         send(rows.at[brick], sums.at[high * 16 + step], 7, g, brick)
+    chunk(b)
     sums[0] = rows[b]
     output[...] = (act_fine + spread(act_all[g, 8:24], pool)).reshape(2, 4, 16, CH)
     arrived(7)
@@ -340,7 +355,7 @@
     for m in FAR_FIRST:
         send(fin.at[g], fin.at[g], 8, mates[m], b)
 
-    for phase in (0, 1, 2, 3, 4, 5, 6, 7, 9):
+    for phase in (0, 1, 2, 3, 4, 5, 6, 7, 9, 10):
         sent(phase)
 
     arrived(8)
@@ -394,8 +409,10 @@
             pltpu.VMEM((GROUPS, 32, CH), F32),
             pltpu.VMEM((8, 2, 4, 8, CH), F32),
             pltpu.VMEM((GROUPS + 2, 3, 16, CH), BF16),
-            pltpu.VMEM((4, 32, 384), BF16),
-            pltpu.VMEM((8, 32, 384), BF16),
+            pltpu.VMEM((4, 32, 128), BF16),
+            pltpu.VMEM((8, 32, 128), BF16),
+            pltpu.VMEM((4, 32, 256), BF16),
+            pltpu.VMEM((8, 32, 256), BF16),
             pltpu.VMEM((PART, 384, 256), BF16),
             pltpu.VMEM((8, 128, CH), BF16),
             pltpu.VMEM((8, 128, CH), BF16),
@@ -409,8 +426,8 @@
             pltpu.VMEM((BRICKS, 16, CH), BF16),
             pltpu.VMEM((GROUPS, 16, CH), F32),
             pltpu.SemaphoreType.DMA((4,)),
-            pltpu.SemaphoreType.DMA((10,)),
-            pltpu.SemaphoreType.DMA((10,)),
+            pltpu.SemaphoreType.DMA((11,)),
+            pltpu.SemaphoreType.DMA((11,)),
             pltpu.SemaphoreType.REGULAR((2,)),
         ],
         compiler_params=pltpu.CompilerParams(

time: 49.3 us -> 49 us (level)
  no operation moved by 1% of the time
where the time goes in v7:
time: 49 us; the launch traced here: 48.9 us
  Pallas kernels  48.2 us (98%)
  between operations  0.64 us (1%)
    pallas_call x1, Pallas kernels, body(): pl.pallas_call(kernel, out_shape=tuple((pltpu.VMEM(shape.shape, shape.dty...  47.6 us

profile of v7, /device:TPU:1, one launch (start us, length us, event | category | flops | bytes accessed | tf_op | source)
XLA Modules:
  0.0 48.9 jit_solution(7806785406701088045)
XLA Ops:
  0.6 47.6 %unet_levels.1 = (f32[2,4,16,128]{3,2,1,0:T(8,128)S(1)}, f32[27,4,128]{2,1,0:T(4,128)S(1)}, f32[27,4,128]{2,1,0:T(4,128)S(1)}) custom-call(f32[2,4,16,128]{3,2,1,0:T(8,128)} %field.1, f32[2,4,16,128]{3,2,1,0:T(8,128)} %cot.1, bf16[9,384,128]{2,1,0:T(8,128)(2,1)} %bitcast.2, bf16[9,384,128]{2,1,0:T(8,128)(2,1)} %bitcast.3), custom_call_target="tpu_custom_call" | custom-call | flops 600000000 | bytes 2500000 | tf_op jit(solution)/shard_map/unet_levels/pallas_call | solution.py:393
  48.2 0.7 %copy_out.1 = (f32[2,4,16,128]{3,2,1,0:T(8,128)}, f32[27,4,128]{2,1,0:T(4,128)}, f32[27,4,128]{2,1,0:T(4,128)}) custom-call(f32[2,4,16,128]{3,2,1,0:T(8,128)S(1)} %get-tuple-element.6.output, f32[27,4,128]{2,1,0:T(4,128)S(1)} %get-tuple-element.7.grad_fine, f32[27,4,128]{2,1,0:T(4,128)S(1)} %get-tuple-element.8.grad_coarse), custom_call_target="tpu_custom_call" | custom-call | tf_op jit(solution)/shard_map/copy_out/pallas_call | solution.py:439

commit v8 on v7

--- a/solution.py
+++ b/solution.py
@@ -351,7 +351,7 @@
     sums[0] = rows[b]
     output[...] = (act_fine + spread(act_all[g, 8:24], pool)).reshape(2, 4, 16, CH)
     arrived(7)
-    fin[g] = jnp.sum(sums[...].astype(F32), axis=0)
+    fin[g] = jnp.sum(sums[...].astype(F32), axis=0).astype(BF16)
     for m in FAR_FIRST:
         send(fin.at[g], fin.at[g], 8, mates[m], b)
 
@@ -363,8 +363,9 @@
         channel, part = member // 4, member % 4
         count = PART if part < 3 else PART - 1
         where = pl.ds(part * PART, count)
-        grad_fine[where, channel, :] = fin[member, 0:count]
-        grad_coarse[where, channel, :] = fin[member, 8 : 8 + count]
+        share_rows = fin[member].astype(F32)
+        grad_fine[where, channel, :] = share_rows[0:count]
+        grad_coarse[where, channel, :] = share_rows[8 : 8 + count]
     sent(8)
 
 
@@ -424,7 +425,7 @@
             pltpu.VMEM((256, CH), F32),
             pltpu.VMEM((BRICKS, 16, CH), BF16),
             pltpu.VMEM((BRICKS, 16, CH), BF16),
-            pltpu.VMEM((GROUPS, 16, CH), F32),
+            pltpu.VMEM((GROUPS, 16, CH), BF16),
             pltpu.SemaphoreType.DMA((4,)),
             pltpu.SemaphoreType.DMA((11,)),
             pltpu.SemaphoreType.DMA((11,)),

time: 49 us -> 49 us (level)
  no operation moved by 1% of the time
where the time goes in v8:
time: 49 us; the launch traced here: 48.8 us
  Pallas kernels  48.2 us (98%)
  between operations  0.64 us (1%)
    pallas_call x1, Pallas kernels, body(): pl.pallas_call(kernel, out_shape=tuple((pltpu.VMEM(shape.shape, shape.dty...  47.5 us

profile of v8, /device:TPU:1, one launch (start us, length us, event | category | flops | bytes accessed | tf_op | source)
XLA Modules:
  0.0 48.8 jit_solution(9777032341786853586)
XLA Ops:
  0.6 47.5 %unet_levels.1 = (f32[2,4,16,128]{3,2,1,0:T(8,128)S(1)}, f32[27,4,128]{2,1,0:T(4,128)S(1)}, f32[27,4,128]{2,1,0:T(4,128)S(1)}) custom-call(f32[2,4,16,128]{3,2,1,0:T(8,128)} %field.1, f32[2,4,16,128]{3,2,1,0:T(8,128)} %cot.1, bf16[9,384,128]{2,1,0:T(8,128)(2,1)} %bitcast.2, bf16[9,384,128]{2,1,0:T(8,128)(2,1)} %bitcast.3), custom_call_target="tpu_custom_call" | custom-call | flops 600000000 | bytes 2500000 | tf_op jit(solution)/shard_map/unet_levels/pallas_call | solution.py:394
  48.1 0.7 %copy_out.1 = (f32[2,4,16,128]{3,2,1,0:T(8,128)}, f32[27,4,128]{2,1,0:T(4,128)}, f32[27,4,128]{2,1,0:T(4,128)}) custom-call(f32[2,4,16,128]{3,2,1,0:T(8,128)S(1)} %get-tuple-element.6.output, f32[27,4,128]{2,1,0:T(4,128)S(1)} %get-tuple-element.7.grad_fine, f32[27,4,128]{2,1,0:T(4,128)S(1)} %get-tuple-element.8.grad_coarse), custom_call_target="tpu_custom_call" | custom-call | tf_op jit(solution)/shard_map/copy_out/pallas_call | solution.py:440

commit v9 on v7

--- a/solution.py
+++ b/solution.py
@@ -359,12 +359,12 @@
         sent(phase)
 
     arrived(8)
-    for member in range(GROUPS):
-        channel, part = member // 4, member % 4
+    for part in range(4):
         count = PART if part < 3 else PART - 1
         where = pl.ds(part * PART, count)
-        grad_fine[where, channel, :] = fin[member, 0:count]
-        grad_coarse[where, channel, :] = fin[member, 8 : 8 + count]
+        shares = [fin[channel * 4 + part] for channel in range(4)]
+        grad_fine[where] = jnp.stack([share[0:count] for share in shares], axis=1)
+        grad_coarse[where] = jnp.stack([share[8 : 8 + count] for share in shares], axis=1)
     sent(8)
 
 

time: 49 us -> 49 us (level)
  no operation moved by 1% of the time
where the time goes in v9:
time: 49 us; the launch traced here: 48.9 us
  Pallas kernels  48.3 us (99%)
  between operations  0.64 us (1%)
    pallas_call x1, Pallas kernels, body(): pl.pallas_call(kernel, out_shape=tuple((pltpu.VMEM(shape.shape, shape.dty...  47.6 us

profile of v9, /device:TPU:1, one launch (start us, length us, event | category | flops | bytes accessed | tf_op | source)
XLA Modules:
  0.0 48.9 jit_solution(17844036829498056327)
XLA Ops:
  0.6 47.6 %unet_levels.1 = (f32[2,4,16,128]{3,2,1,0:T(8,128)S(1)}, f32[27,4,128]{2,1,0:T(4,128)S(1)}, f32[27,4,128]{2,1,0:T(4,128)S(1)}) custom-call(f32[2,4,16,128]{3,2,1,0:T(8,128)} %field.1, f32[2,4,16,128]{3,2,1,0:T(8,128)} %cot.1, bf16[9,384,128]{2,1,0:T(8,128)(2,1)} %bitcast.2, bf16[9,384,128]{2,1,0:T(8,128)(2,1)} %bitcast.3), custom_call_target="tpu_custom_call" | custom-call | flops 600000000 | bytes 2500000 | tf_op jit(solution)/shard_map/unet_levels/pallas_call | solution.py:393
  48.2 0.7 %copy_out.1 = (f32[2,4,16,128]{3,2,1,0:T(8,128)}, f32[27,4,128]{2,1,0:T(4,128)}, f32[27,4,128]{2,1,0:T(4,128)}) custom-call(f32[2,4,16,128]{3,2,1,0:T(8,128)S(1)} %get-tuple-element.6.output, f32[27,4,128]{2,1,0:T(4,128)S(1)} %get-tuple-element.7.grad_fine, f32[27,4,128]{2,1,0:T(4,128)S(1)} %get-tuple-element.8.grad_coarse), custom_call_target="tpu_custom_call" | custom-call | tf_op jit(solution)/shard_map/copy_out/pallas_call | solution.py:439
